TPU v7x, 32 devices: a whole 2x2x4 slice. The times are simulated.
32 devices in a mesh: row: 8 (over z, x), col: 2 (over core), vec: 2 (over y).
Axes of the slice: x: 2, y: 2, z: 4, core: 2. Of those that a mesh axis runs over, the one named last changes fastest.
Arguments:
- vectors: bfloat16 [131072, 256], P(('row', 'col'), 'vec'), parts along dimension 1, may hold values from -6 to 6
- tile_blocks: bfloat16 [8, 2, 32, 256, 256], P('row', 'col'), may hold values from -0.375 to 0.375
- block_rows: int32 [8, 2, 32], P('row', 'col'), may hold values from 0 to 63, as said below
- block_cols: int32 [8, 2, 32], P('row', 'col'), may hold values from 0 to 255, as said below
- counts: int32 [8, 2], P('row', 'col'), may hold values from 1 to 32, as said below
Outputs:
- filtered: bfloat16 [131072, 256], P(('row', 'col'), 'vec'), parts along dimension 1
There are 2 independent parts, one for each index of `vec`. A program takes and returns all parts, laid end to end along the dimension named above; an argument that names none is the same for every part. Nothing has to cross between parts.
Inputs may be any that keep to these rules, and one draw needn't show every extreme that they name: The pairs (block_rows, block_cols // 32) of the 32 slots of one tile are all distinct. Within one tile, all slots whose block columns lie in the same group of 32 (same block_cols // 32) name the same block column. `counts`: some tile uses all 32 slots.
All inputs are finite; a program needn't handle non-finite values.
Results may differ from a plain program's by a relative error of at most 0.015.
Values may be sent and summed in bfloat16 or wider, within the bound.
No kernel may reach another device: no remote copies, remote signals or barrier semaphores. Data moves between devices by JAX's collectives and lax.ppermute only.
A program may use at most 64 MiB of HBM per device.

v0:
```python
import functools
import typing

import jax
import jax.numpy as jnp
from jax import lax
from jax.experimental import pallas as pl
from jax.experimental.pallas import tpu as pltpu
from jax.sharding import PartitionSpec as P

DEGREE = 3

center_value = 0.5
half_width = 2.0

VMEM = pltpu.VMEM
SMEM = pltpu.SMEM
HBM = pltpu.HBM
DMA = pltpu.SemaphoreType.DMA
LANES = 128
FEW = 4
MANY = 4
HEAD = 8
STRIDE = 4
FIRST = 1
LAST = 2


def spec(space):
    return pl.BlockSpec(memory_space=space)


def params(mib):
    return pltpu.CompilerParams(vmem_limit_bytes=mib * 1024 * 1024)


def round_up(n, step):
    return (n + step - 1) // step * step


def core_number():
    return lax.axis_index("col")


class Layout(typing.NamedTuple):
    slots: int
    sends: int
    loads: int
    sent_at: int
    load_at: int
    bare_at: int
    size: int


def layout_for(slot_count, n_row, piece_blocks):
    slots = round_up(slot_count, MANY) + MANY
    sends = round_up(2 * n_row * n_row, FEW) + FEW
    sent_at = HEAD + STRIDE * 2 * slots
    load_at = sent_at + STRIDE * 2 * sends
    bare_at = load_at + 2 * (slot_count + 1)
    size = round_up(bare_at + piece_blocks, 8 * LANES)
    return Layout(slots, sends, slot_count + 1, sent_at, load_at, bare_at, size)


def plan_kernel(
    n_row,
    piece_blocks,
    lay,
    wanted_a,
    wanted_b,
    meta_a,
    meta_b,
    own,
    other,
    out,
    asked,
    seen,
    sems,
):
    slot_count = (meta_a.shape[0] - 1) // 2

    def put(at, *values):
        for i, value in enumerate(values):
            out[at + i] = value

    def scan(tile, meta):
        used = meta[2 * slot_count]


        def step(s, carry):
            ends, sent, load = carry
            row = meta[s]
            piece = meta[slot_count + s] // piece_blocks
            live = s < used
            half = row // piece_blocks
            local = row - half * piece_blocks
            lower = half == 0
            part = jnp.where(lower, tile, 1 - tile)
            at = HEAD + STRIDE * (part * lay.slots + jnp.where(lower, ends[0], ends[1]))
            base = half * lay.size
            put(base + at, s, local, piece)
            sought = jnp.where(live, local, -1)
            hits = [(asked[half * n_row + k] == sought).astype(jnp.int32) for k in range(n_row)]
            found = sum(hits)

            @pl.when(found > 0)
            def _():
                for core in range(2):
                    mine = tile if core == 0 else 1 - tile
                    side = half if core == 0 else 1 - half
                    first = core * lay.size
                    out[first + lay.load_at + mine * lay.loads + load] = s

                    place = sent
                    for k in range(n_row):
                        put(
                            first + lay.sent_at + STRIDE * (mine * lay.sends + place),
                            mine * lay.loads + load,
                            2 * k + side,
                            piece,
                            jnp.where(place == sent, FIRST, 0),
                        )
                        place = place + hits[k]

            one = live.astype(jnp.int32)
            ends = (ends[0] + jnp.where(lower, one, 0), ends[1] + jnp.where(lower, 0, one))
            return ends, sent + found, load + jnp.where(found > 0, 1, 0)

        zero = jnp.int32(0)
        ends, sent, load = lax.fori_loop(0, slot_count, step, ((zero, zero), zero, zero))
        for core in range(2):
            mine = tile if core == 0 else 1 - tile
            base = core * lay.size
            for i, (at, begin, end, unit, spare) in enumerate(
                (
                    (HEAD, mine * lay.slots, ends[core], MANY, piece_blocks),
                    (lay.sent_at, mine * lay.sends, sent, FEW, 2 * n_row),
                )
            ):
                for u in range(unit - 1):
                    put(base + at + STRIDE * (begin + end + u), 0, spare, 0, 0)
                out[base + 2 * i + mine] = begin + (end + unit - 1) // unit * unit
            out[base + 4 + mine] = mine * lay.loads + load

    def mark(core):
        base = core * lay.size
        for b in range(piece_blocks + 1):
            seen[b] = 0
        for part in range(2):

            @pl.loop(part * lay.slots, out[base + part])
            def _(i):
                entry = base + HEAD + STRIDE * i
                row = out[entry + 1]
                out[entry + 3] = jnp.where(seen[row] == 0, FIRST, 0)
                seen[row] = entry

        def close(b, bare):
            entry = seen[b]
            out[base + lay.bare_at + bare] = b

            @pl.when(entry > 0)
            def _():
                out[entry + 3] = out[entry + 3] + LAST

            return bare + jnp.where(entry == 0, 1, 0)

        out[base + 6] = lax.fori_loop(0, piece_blocks, close, jnp.int32(0))
        out[base + 7] = core

    @pl.when(core_number() == 0)
    def _():
        for half, wanted in enumerate((wanted_a, wanted_b)):
            for k in range(n_row):
                asked[half * n_row + k] = wanted[k, 0]
        scan(0, meta_a)
        scan(1, meta_b)
        for core in range(2):
            mark(core)
        copies = [
            pltpu.make_async_copy(out.at[pl.ds(core * lay.size, lay.size)], target, sems.at[core])
            for core, target in enumerate((own, other))
        ]
        for copy in copies:
            copy.start()
        for copy in copies:
            copy.wait()


def settle_kernel(own, handed, out, sem):
    for half, source in enumerate((own, handed)):

        @pl.when(core_number() == half)
        def _():
            copy = pltpu.make_async_copy(source, out, sem)
            copy.start()
            copy.wait()


def pick_kernel(n_row, block_size, wanted, vectors, out, sems):
    def fetch(k):
        at = pl.multiple_of(wanted[k, 0] * block_size, block_size)
        return pltpu.make_async_copy(vectors.at[pl.ds(at, block_size)], out.at[k], sems.at[k])

    for k in range(n_row):
        fetch(k).start()
    for k in range(n_row):
        fetch(k).wait()


def pack_kernel(picked, picked_b, out, held, sems):
    n_row, _, width = picked.shape
    middle = width // 2

    def put(k):
        return pltpu.make_async_copy(held.at[k], out.at[k], sems.at[k])

    for half in range(2):

        @pl.when(core_number() == half)
        def _():
            part = slice(half * middle, (half + 1) * middle)
            for k in range(n_row):
                held[k] = jnp.concatenate([picked[k, :, part], picked_b[k, :, part]], axis=1)
                put(k).start()

    for k in range(n_row):
        put(k).wait()


def fetches(plan, base, stride, ends, part, tiles, blocks, sems):
    def copy(tile, i):
        slot = plan[base + stride * i]
        return pltpu.make_async_copy(tile.at[slot], blocks.at[i], sems.at[i])

    def start():
        for side, tile in enumerate(tiles):

            @pl.loop(side * part, plan[ends + side])
            def _(i):
                copy(tile, i).start()

    def wait(i):
        copy(tiles[0], i).wait()

    return start, wait


def load_kernel(plan, tile_a, array, blocks, held, sems, held_sem):
    whole = pltpu.make_async_copy(array, held, held_sem)
    whole.start()
    start, wait = fetches(plan, HEAD, STRIDE, 0, 0, (tile_a,), blocks, sems)
    start()

    @pl.loop(0, plan[0])
    def _(i):
        wait(i)

    whole.wait()


def each_product(plan, base, ends, part, block_of, pieces, use, then=None, before=None):
    unroll = MANY if base == HEAD else FEW

    for side in range(2):

        @pl.loop(side * part // unroll, plan[ends + side] // unroll)
        def _(j):
            step = [(unroll * j + u, base + STRIDE * (unroll * j + u)) for u in range(unroll)]
            if before is not None:
                for i, entry in step:
                    before(side, i, entry)
            for i, entry in step:
                block = block_of(side, i, entry)
                piece = pieces[side][plan[entry + 2]]
                use(entry, jnp.dot(block, piece, preferred_element_type=jnp.float32))
            if then is not None:
                for i, entry in step:
                    then(entry)


def add_products(plan, base, ends, part, block_of, pieces, total, before=None):
    def use(entry, value):
        total[plan[entry + 1]] += value

    each_product(plan, base, ends, part, block_of, pieces, use, before=before)


def split_sides(pieces, vec):
    middle = vec.shape[-1] // 2
    column = lax.broadcasted_iota(jnp.int32, (1, vec.shape[-1]), 1)
    for side in range(2):
        keep = jnp.where((column // middle) == side, 1.0, 0.0).astype(jnp.bfloat16)
        for p in range(vec.shape[1]):
            vec[side, p] = pieces[p] * keep


def joined(total, k):
    one, two = total[2 * k], total[2 * k + 1]
    low = lax.broadcasted_iota(jnp.int32, one.shape, 1) < one.shape[1] // 2
    return jnp.where(low, one, two) + pltpu.roll(
        jnp.where(low, two, one), one.shape[1] // 2, axis=1
    )


def first_sent_kernel(
    lay, plan, tile_a, tile_b, pieces, start, out, blocks, vec, total, held, held_sem, sems
):
    n_row = out.shape[0]
    begin, wait = fetches(plan, lay.load_at, 1, 4, lay.loads, (tile_a, tile_b), blocks, sems)
    begin()
    copy = pltpu.make_async_copy(start, held, held_sem)
    copy.start()
    split_sides(pieces, vec)
    total[...] = jnp.zeros_like(total)

    def before(side, i, entry):
        @pl.when(plan[entry + 3] == FIRST)
        def _():
            wait(plan[entry])

    add_products(
        plan,
        lay.sent_at,
        2,
        lay.sends,
        lambda side, i, entry: blocks[plan[entry]],
        (vec.at[0], vec.at[1]),
        total,
        before,
    )
    copy.wait()
    for k in range(n_row):
        value = joined(total, k) - center_value * held[k].astype(jnp.float32)
        out[k] = (value / half_width).astype(jnp.bfloat16)


def second_sent_kernel(
    lay, plan, blocks, pieces, current, previous, out, vec, total, held, held_sem, ready, out_sems
):
    n_row = out.shape[0]
    copy = pltpu.make_async_copy(previous, held, held_sem)
    copy.start()
    split_sides(pieces, vec)
    total[...] = jnp.zeros_like(total)
    add_products(
        plan,
        lay.sent_at,
        2,
        lay.sends,
        lambda side, i, entry: blocks[plan[entry]],
        (vec.at[0], vec.at[1]),
        total,
    )
    copy.wait()

    def put(k):
        return pltpu.make_async_copy(ready.at[k], out.at[k], out_sems.at[k])

    for k in range(n_row):
        value = joined(total, k) - center_value * current[k].astype(jnp.float32)
        ready[k] = (value - held[k].astype(jnp.float32)).astype(jnp.bfloat16)
        put(k).start()
    for k in range(n_row):
        put(k).wait()


def whole_columns(half, mine, other, vec, at):
    n_row, _, width = mine.shape
    middle = width // 2

    @pl.when(half == 0)
    def _():
        for p in range(n_row):
            one, two = mine[p], other[p]
            vec[0, p, :, at : at + width] = jnp.concatenate([one[:, :middle], two[:, middle:]], axis=1)
            vec[1, p, :, at : at + width] = jnp.concatenate([one[:, middle:], two[:, :middle]], axis=1)

    @pl.when(half != 0)
    def _():
        for p in range(n_row):
            one, two = mine[p], other[p]
            vec[0, p, :, at : at + width] = jnp.concatenate([two[:, middle:], one[:, :middle]], axis=1)
            vec[1, p, :, at : at + width] = jnp.concatenate([two[:, :middle], one[:, middle:]], axis=1)


def prime_kernel(vectors, total, own, sem):
    _, block_size, double = total.shape
    width = double // 2
    copy = pltpu.make_async_copy(vectors, own, sem)
    copy.start()
    copy.wait()

    @pl.loop(0, vectors.shape[0] // block_size)
    def _(b):
        at = pl.ds(pl.multiple_of(b * block_size, block_size), block_size)
        value = own[at, :].astype(jnp.float32)
        total[b, :, :width] = -center_value * value
        total[b, :, width:] = -value


def early_kernel(
    lay,
    plan,
    tile_a,
    tile_b,
    q1,
    q1_other,
    q2,
    q2_other,
    start,
    base,
    total,
    vec,
    own,
    blocks,
    sems,
    row_sems,
):
    piece_blocks, block_size, width = base.shape
    begin, wait = fetches(plan, HEAD, STRIDE, 0, lay.slots, (tile_a, tile_b), blocks, sems)
    begin()
    whole_columns(plan[7], q1, q1_other, vec, 0)
    whole_columns(plan[7], q2, q2_other, vec, width)

    def rows(b):
        return pl.ds(pl.multiple_of(b * block_size, block_size), block_size)

    def put(b):
        return pltpu.make_async_copy(own.at[rows(b)], base.at[b], row_sems.at[b])

    add_products(
        plan,
        HEAD,
        0,
        lay.slots,
        lambda side, i, entry: blocks[i],
        (vec.at[0], vec.at[1]),
        total,
        lambda side, i, entry: wait(i),
    )

    @pl.loop(0, piece_blocks)
    def _(b):
        first = (total[b, :, :width] / half_width).astype(jnp.bfloat16).astype(jnp.float32)
        second = total[b, :, width:] - center_value * first
        second = second.astype(jnp.bfloat16).astype(jnp.float32)
        own[rows(b), :] = (-center_value * second - first).astype(jnp.bfloat16)
        put(b).start()

    @pl.loop(0, piece_blocks)
    def _(b):
        put(b).wait()


def last_kernel(
    lay, plan, blocks, tile_b, mine, other, base, out, vec, total, own, blocks_b, sems, row_sems
):
    piece_blocks = base.shape[0]
    begin = lay.slots

    def fetch(i):
        slot = plan[HEAD + STRIDE * i]
        return pltpu.make_async_copy(tile_b.at[slot], blocks_b.at[i - begin], sems.at[i - begin])

    @pl.loop(begin, plan[1])
    def _(i):
        fetch(i).start()

    def put(source, b):
        return pltpu.make_async_copy(source.at[b], out.at[b], row_sems.at[b])

    @pl.loop(0, plan[6])
    def _(i):
        b = plan[lay.bare_at + i]
        put(base, b).start()

    whole_columns(plan[7], mine, other, vec, 0)

    def use(entry, value):
        row = plan[entry + 1]
        marks = plan[entry + 3]
        start = base[jnp.minimum(row, piece_blocks - 1)].astype(jnp.float32)
        value = jnp.where(lax.rem(marks, LAST) == FIRST, start, total[row]) + value
        total[row] = value
        own[row] = value.astype(jnp.bfloat16)

    def then(entry):
        @pl.when(plan[entry + 3] >= LAST)
        def _():
            put(own, plan[entry + 1]).start()

    def block_of(side, i, entry):
        return blocks[i] if side == 0 else blocks_b[i - begin]

    def before(side, i, entry):
        if side == 1:
            fetch(i).wait()

    each_product(
        plan, HEAD, 0, lay.slots, block_of, (vec.at[0], vec.at[1]), use, then, before
    )

    @pl.loop(0, piece_blocks)
    def _(b):
        put(own, b).wait()


def after(value, *others):
    return lax.optimization_barrier((value, *others))[0]


def call(kernel, out, args, spaces, scratch, mib, name, estimate=None, aliases=None):
    args = [
        pltpu.with_memory_space_constraint(arg, space) if space in (VMEM, HBM) or tied else arg
        for arg, (space, tied) in zip(args, spaces)
    ]
    return pl.pallas_call(
        kernel,
        out_shape=[space(shape, dtype) for shape, dtype, space in out],
        in_specs=[spec(space) for space, _ in spaces],
        out_specs=[spec(space) for _, _, space in out],
        scratch_shapes=scratch,
        compiler_params=params(mib),
        cost_estimate=estimate,
        input_output_aliases=aliases or {},
        name=name,
    )(*args)


HERE = (VMEM, True)
FAR = (HBM, True)
LIST = (SMEM, True)
SCALARS = (SMEM, False)
ANYWHERE = (pl.ANY, False)


def on_pair(vectors, tile_blocks, block_rows, block_cols, counts):
    n_row = lax.axis_size("row")
    tile = tile_blocks[0, 0]
    slot_rows = block_rows[0, 0]
    slot_cols = block_cols[0, 0]
    used = counts[0]
    slot_count, block_size, _ = tile.shape
    width = vectors.shape[1]
    piece_blocks = vectors.shape[0] // block_size

    across = functools.partial(lax.ppermute, axis_name="col", perm=[(0, 1), (1, 0)])

    needed = jnp.max(
        jnp.where(
            slot_cols[None, :] // piece_blocks == jnp.arange(n_row)[:, None],
            slot_cols[None, :] % piece_blocks,
            0,
        ),
        axis=1,
        keepdims=True,
    )
    exchange = functools.partial(
        lax.all_to_all, axis_name="row", split_axis=0, concat_axis=0, tiled=True
    )
    wanted = exchange(jnp.broadcast_to(needed, (n_row, LANES)))
    sent_shape = (n_row, block_size, width)
    (sent,) = call(
        functools.partial(pick_kernel, n_row, block_size),
        [(sent_shape, jnp.bfloat16, VMEM)],
        (wanted, vectors),
        (SCALARS, FAR),
        [DMA((n_row,))],
        2,
        "pick",
    )
    tile_other = across(tile)
    sent_other = across(sent)
    wanted_other = across(after(wanted, sent))
    meta = jnp.concatenate([slot_rows, slot_cols, used])
    meta_other = across(after(meta, sent))
    packed = call(
        pack_kernel,
        [(sent_shape, jnp.bfloat16, HBM)],
        (sent, sent_other),
        (HERE, HERE),
        [VMEM(sent_shape, jnp.bfloat16), DMA((n_row,))],
        4,
        "pack",
    )[0]

    lay = layout_for(slot_count, n_row, piece_blocks)
    list_shape = ((lay.size,), jnp.int32)
    own_list, other_list = call(
        functools.partial(plan_kernel, n_row, piece_blocks, lay),
        [(*list_shape, HBM)] * 2,
        (wanted, after(wanted_other, packed), meta, meta_other),
        (SCALARS,) * 4,
        [
            SMEM((2 * lay.size,), jnp.int32),
            SMEM((2 * n_row,), jnp.int32),
            SMEM((piece_blocks + 1,), jnp.int32),
            DMA((2,)),
        ],
        2,
        "plan",
    )
    q1 = exchange(after(packed, own_list))
    plan = call(
        settle_kernel,
        [(*list_shape, SMEM)],
        (own_list, across(after(other_list, packed))),
        (ANYWHERE, ANYWHERE),
        [DMA],
        2,
        "settle",
    )[0]

    def load(cue, array):
        return call(
            load_kernel,
            [
                ((lay.slots, block_size, block_size), jnp.bfloat16, VMEM),
                (array.shape, array.dtype, VMEM),
            ],
            (after(plan, cue), tile, array),
            (LIST, FAR, FAR),
            [DMA((lay.slots,)), DMA],
            2,
            "load",
        )

    def cost(products, rows):
        size = block_size * width
        return pl.CostEstimate(
            flops=2 * products * block_size * size,
            bytes_accessed=2 * (products * block_size * block_size + 3 * rows * size),
            transcendentals=0,
        )

    sums = [
        VMEM((2, n_row, block_size, width), jnp.bfloat16),
        VMEM((2 * n_row + 1, block_size, width), jnp.float32),
    ]

    def first_blocks(*args):
        return call(
            functools.partial(first_sent_kernel, lay),
            [
                (sent_shape, jnp.bfloat16, VMEM),
                ((2 * lay.loads, block_size, block_size), jnp.bfloat16, VMEM),
            ],
            (plan, tile, tile_other, *args),
            (LIST, FAR, ANYWHERE, HERE, FAR),
            sums + [VMEM(sent_shape, jnp.bfloat16), DMA, DMA((2 * lay.loads,))],
            8,
            "sent",
            cost(n_row, n_row),
        )

    def second_blocks(*args):
        return call(
            functools.partial(second_sent_kernel, lay),
            [(sent_shape, jnp.bfloat16, HBM)],
            (plan, *args),
            (LIST, HERE, HERE, HERE, FAR),
            sums
            + [VMEM(sent_shape, jnp.bfloat16), DMA, VMEM(sent_shape, jnp.bfloat16), DMA((n_row,))],
            8,
            "sent",
            cost(n_row, n_row),
        )[0]

    base_shape = (piece_blocks, block_size, width)

    sums_shape = ((piece_blocks + 1, block_size, 2 * width), jnp.float32, VMEM)

    def early(*args):
        return call(
            functools.partial(early_kernel, lay),
            [(base_shape, jnp.bfloat16, HBM), sums_shape],
            (plan, tile, tile_other, *args),
            (LIST, FAR, ANYWHERE, HERE, HERE, HERE, HERE, HERE),
            [
                VMEM((2, n_row, block_size, 2 * width), jnp.bfloat16),
                VMEM(vectors.shape, jnp.bfloat16),
                VMEM((2 * lay.slots, block_size, block_size), jnp.bfloat16),
                DMA((2 * lay.slots,)),
                DMA((piece_blocks,)),
            ],
            18,
            "early",
            cost(2 * slot_count, 2 * piece_blocks),
            {7: 1},
        )[0]

    def last(blocks, *args):
        rows = (piece_blocks + 1, block_size, width)
        (out,) = call(
            functools.partial(last_kernel, lay),
            [(base_shape, jnp.bfloat16, HBM)],
            (plan, blocks, tile_other, *args),
            (LIST, HERE, ANYWHERE, HERE, HERE, HERE),
            [
                VMEM((2, n_row, block_size, width), jnp.bfloat16),
                VMEM(rows, jnp.float32),
                VMEM(rows, jnp.bfloat16),
                VMEM((lay.slots, block_size, block_size), jnp.bfloat16),
                DMA((lay.slots,)),
                DMA((piece_blocks,)),
            ],
            14,
            "last",
            cost(slot_count, piece_blocks),
        )
        return out.reshape(vectors.shape)

    q1 = after(q1, plan)
    first_sent, blocks = first_blocks(q1, packed)
    q2 = exchange(first_sent)
    second_sent = second_blocks(blocks, q2, first_sent, packed)
    q1_other = across(after(q1, second_sent))
    q2_other = across(after(q2, second_sent))
    (start,) = call(
        prime_kernel,
        [sums_shape],
        (after(vectors, second_sent),),
        (FAR,),
        [VMEM(vectors.shape, jnp.bfloat16), DMA],
        4,
        "prime",
        cost(0, 3 * piece_blocks),
    )
    base = early(q1, q1_other, q2, q2_other, start)
    q3 = after(exchange(second_sent), base)
    q3_other = across(q3)
    blocks, base = load(q3, base)
    return last(blocks, q3, q3_other, base)


def on_any(vectors, tile_blocks, block_rows, block_cols, counts):
    n_row = lax.axis_size("row")
    n_col = lax.axis_size("col")
    tile_data = tile_blocks[0, 0]
    slot_rows = block_rows[0, 0]
    slot_cols = block_cols[0, 0]
    used = counts[0, 0]
    block_size = tile_data.shape[-1]
    width = vectors.shape[1]
    piece_blocks = vectors.shape[0] // block_size
    row_blocks = piece_blocks * n_col
    slot_count = tile_data.shape[0]
    live = (jnp.arange(slot_count) < used).astype(jnp.float32)
    onehot = (slot_rows[None, :] == jnp.arange(row_blocks)[:, None]).astype(jnp.float32) * live[
        None, :
    ]
    source_piece = slot_cols // piece_blocks
    offset = slot_cols % piece_blocks
    needed = jnp.max(
        jnp.where(source_piece[None, :] == jnp.arange(n_row)[:, None], offset[None, :], 0), axis=1
    )
    wanted = lax.all_to_all(
        needed.reshape(n_row, 1), "row", split_axis=0, concat_axis=0, tiled=True
    ).reshape(n_row)

    def apply_tiles(current):
        own_blocks = current.reshape(piece_blocks, block_size, width)
        outgoing = jnp.take(own_blocks, wanted, axis=0)
        received = lax.all_to_all(outgoing, "row", split_axis=0, concat_axis=0, tiled=True)
        vec_blocks = jnp.take(received, source_piece, axis=0)
        products = jnp.einsum(
            "sij,sjk->sik", tile_data, vec_blocks, preferred_element_type=jnp.float32
        )
        term = jnp.einsum("ls,sik->lik", onehot, products, precision=lax.Precision.HIGHEST)
        term = term.reshape(row_blocks * block_size, width)
        return lax.psum_scatter(
            term.astype(jnp.bfloat16), "col", scatter_dimension=0, tiled=True
        ).astype(jnp.float32)

    previous = vectors
    applied = apply_tiles(vectors)
    current = ((applied - center_value * previous.astype(jnp.float32)) / half_width).astype(
        jnp.bfloat16
    )
    for repeat in range(DEGREE - 1):
        applied = apply_tiles(current)
        following = (
            2.0 * (applied - center_value * current.astype(jnp.float32)) / half_width
            - previous.astype(jnp.float32)
        ).astype(jnp.bfloat16)
        previous, current = (current, following)
    return current


def solution(mesh):
    n_row, n_col = mesh.shape["row"], mesh.shape["col"]
    paired = n_col == 2 and n_row & (n_row - 1) == 0
    return jax.shard_map(
        on_pair if paired else on_any,
        mesh=mesh,
        in_specs=(
            P(("row", "col"), "vec"),
            P("row", "col", None, None, None),
            P("row", "col", None),
            P("row", "col", None),
            P("row", "col"),
        ),
        out_specs=P(("row", "col"), "vec"),
        check_vma=False,
    )
```

profile of v0, /device:TPU:0, one launch (start us, length us, event | category | flops | bytes accessed | tf_op | source)
XLA Modules:
  0.0 79.1 jit_solution(15092019712727004471)
XLA Ops:
  0.0 0.5 collective-permute-start.4
  0.5 0.7 and_select_fusion.1
  1.3 13.1 %all_to_all.23 = s32[8,1,128]{2,1,0:T(1,128)S(1)} all-to-all(s32[8,1,128]{2,1,0:T(1,128)S(1)} %broadcast_in_dim.21), channel_id=1, replica_groups=mesh['row'=8,'col'=2,'vec'=2] {'row'}, dimensions={0} | all-to-all | bytes 8192 | tf_op jit(solution)/shard_map/all_to_all | solution.py:562
  14.4 1.7 %pick.1.picked = bf16[8,256,128]{2,1,0:T(8,128)(2,1)S(1)} custom-call(s32[8,128]{1,0:T(8,128)S(1)} %bitcast.13, bf16[8192,128]{1,0:T(8,128)(2,1)} %vectors.2), custom_call_target="tpu_custom_call" | custom-call | tf_op jit(solution)/shard_map/pick/pallas_call | solution.py:518
  16.8 0.6 collective-permute-start
  17.4 0.7 pad_add_fusion.meta_a
  18.2 0.9 %pack.1.start.previous = bf16[8,256,128]{2,1,0:T(8,128)(2,1)} custom-call(bf16[8,256,128]{2,1,0:T(8,128)(2,1)S(1)} %pick.1.picked, bf16[8,256,128]{2,1,0:T(8,128)(2,1)S(1)} %collective-permute-done.1.picked_b), custom_call_target="tpu_custom_call" | custom-call | tf_op jit(solution)/shard_map/pack/pallas_call | solution.py:518
  19.1 0.1 collective-permute-done.2.meta_b
  19.3 6.5 %plan.1 = (s32[2048]{0:T(1024)}, s32[2048]{0:T(1024)}) custom-call(s32[8,128]{1,0:T(8,128)S(1)} %bitcast.15, s32[8,128]{1,0:T(8,128)S(1)} %collective-permute-done.wanted_b, s32[65]{0:T(128)S(1)} %pad_add_fusion.meta_a, s32[65]{0:T(128)S(1)} %collective-permute-done.2.meta_b), custom_call_target="tpu_custom_call" | custom-call | tf_op jit(solution)/shard_map/plan/pallas_call | solution.py:518
  25.8 3.5 %all-to-all-start.1 = ((bf16[8,256,128]{2,1,0:T(8,128)(2,1)}), bf16[8,256,128]{2,1,0:T(8,128)(2,1)S(1)}, u32[]{:S(2)}, u32[]{:S(2)}) async-start(bf16[8,256,128]{2,1,0:T(8,128)(2,1)} %pack.1.start.previous), calls=%async_computation.1 | async-start | bytes 1048576 | tf_op jit(solution)/shard_map/all_to_all | solution.py:604
  29.4 1.4 %collective-permute-done.3.handed = s32[2048]{0:T(1024)S(1)} collective-permute-done((s32[2048]{0:T(1024)}, s32[2048]{0:T(1024)S(1)}, u32[]{:S(2)}, u32[]{:S(2)}) %collective-permute-start.3) | collective-permute-done | bytes 8224 | tf_op jit(solution)/shard_map/ppermute | solution.py:608
  30.8 0.7 copy-done
  31.5 0.7 settle.1.plan
  32.2 7.4 %all-to-all-done.1.pieces.q1 = bf16[8,256,128]{2,1,0:T(8,128)(2,1)S(1)} async-done(((bf16[8,256,128]{2,1,0:T(8,128)(2,1)}), bf16[8,256,128]{2,1,0:T(8,128)(2,1)S(1)}, u32[]{:S(2)}, u32[]{:S(2)}) %all-to-all-start.1) | async-done | bytes 524320 | tf_op jit(solution)/shard_map/all_to_all | solution.py:604
  39.5 3.9 %sent.2 = (bf16[8,256,128]{2,1,0:T(8,128)(2,1)S(1)}, bf16[66,256,256]{2,1,0:T(8,128)(2,1)S(1)}) custom-call(s32[2048]{0:T(1024)S(4)} %settle.1.plan, bf16[32,256,256]{2,1,0:T(8,128)(2,1)} %bitcast.17, bf16[32,256,256]{2,1,0:T(8,128)(2,1)} %collective-permute-done.4.tile_b, bf16[8,256,128]{2,1,0:T(8,128)(2,1)S(1)} %all-to-all-done.1.pieces.q1, ...), custom_call_target="tpu_custom_call" | custom-call | flops 134217728 | bytes 2621440 | tf_op jit(solution)/shard_map/sent/pallas_call | solution.py:518
  43.4 12.7 %all_to_all.24.pieces.q2 = bf16[8,256,128]{2,1,0:T(8,128)(2,1)S(1)} all-to-all(bf16[8,256,128]{2,1,0:T(8,128)(2,1)S(1)} %get-tuple-element.32.current), channel_id=1, replica_groups=mesh['row'=8,'col'=2,'vec'=2] {'row'}, dimensions={0} | all-to-all | bytes 1048576 | tf_op jit(solution)/shard_map/all_to_all | solution.py:716
  56.2 3.1 %sent.3 = bf16[8,256,128]{2,1,0:T(8,128)(2,1)} custom-call(s32[2048]{0:T(1024)S(4)} %settle.1.plan, bf16[66,256,256]{2,1,0:T(8,128)(2,1)S(1)} %get-tuple-element.31.blocks, bf16[8,256,128]{2,1,0:T(8,128)(2,1)S(1)} %all_to_all.24.pieces.q2, bf16[8,256,128]{2,1,0:T(8,128)(2,1)S(1)} %get-tuple-element.32.current, bf16[8,256,128]{2,1,0:T(8,128)(2,1)} %pack.1.start.previous), custom_call_target="tpu_custom_call" | custom-call | flops 134217728 | bytes 2621440 | tf_op jit(solution)/shard_map/sent/pallas_call | solution.py:518
  59.3 3.5 %all-to-all-start.3 = ((bf16[8,256,128]{2,1,0:T(8,128)(2,1)}), bf16[8,256,128]{2,1,0:T(8,128)(2,1)S(1)}, u32[]{:S(2)}, u32[]{:S(2)}) async-start(bf16[8,256,128]{2,1,0:T(8,128)(2,1)} %sent.3), calls=%async_computation.3 | async-start | bytes 1048576 | tf_op jit(solution)/shard_map/all_to_all | solution.py:731
  62.9 0.5 collective-permute-start.6
  63.4 2.3 %prime.1.start = f32[33,256,256]{2,1,0:T(8,128)S(1)} custom-call(bf16[8192,128]{1,0:T(8,128)(2,1)} %vectors.2), custom_call_target="tpu_custom_call" | custom-call | bytes 18874368 | tf_op jit(solution)/shard_map/prime/pallas_call | solution.py:518
  65.7 5.8 %early.1 = (bf16[32,256,128]{2,1,0:T(8,128)(2,1)}, f32[33,256,256]{2,1,0:T(8,128)S(1)}) custom-call(s32[2048]{0:T(1024)S(4)} %settle.1.plan, bf16[32,256,256]{2,1,0:T(8,128)(2,1)} %bitcast.18, bf16[32,256,256]{2,1,0:T(8,128)(2,1)} %collective-permute-done.4.tile_b, ...), custom_call_target="tpu_custom_call", output_to_operand_aliasing={{1}: (7, {})} | custom-call | flops 1073741824 | bytes 20971520 | tf_op jit(solution)/shard_map/early/pallas_call | solution.py:518
  71.5 1.5 %all-to-all-done.3.mine = bf16[8,256,128]{2,1,0:T(8,128)(2,1)S(1)} async-done(((bf16[8,256,128]{2,1,0:T(8,128)(2,1)}), bf16[8,256,128]{2,1,0:T(8,128)(2,1)S(1)}, u32[]{:S(2)}, u32[]{:S(2)}) %all-to-all-start.3) | async-done | bytes 524320 | tf_op jit(solution)/shard_map/all_to_all | solution.py:731
  73.0 2.0 %load.1 = (bf16[36,256,256]{2,1,0:T(8,128)(2,1)S(1)}, bf16[32,256,128]{2,1,0:T(8,128)(2,1)S(1)}) custom-call(s32[2048]{0:T(1024)S(4)} %settle.1.plan, bf16[32,256,256]{2,1,0:T(8,128)(2,1)} %bitcast.19, bf16[32,256,128]{2,1,0:T(8,128)(2,1)} %get-tuple-element.36.array), custom_call_target="tpu_custom_call" | custom-call | tf_op jit(solution)/shard_map/load/pallas_call | solution.py:518
  75.0 4.1 %last.1 = bf16[32,256,128]{2,1,0:T(8,128)(2,1)} custom-call(s32[2048]{0:T(1024)S(4)} %settle.1.plan, bf16[36,256,256]{2,1,0:T(8,128)(2,1)S(1)} %get-tuple-element.39.blocks, bf16[32,256,256]{2,1,0:T(8,128)(2,1)} %collective-permute-done.4.tile_b, bf16[8,256,128]{2,1,0:T(8,128)(2,1)S(1)} %all-to-all-done.3.mine, ...), custom_call_target="tpu_custom_call" | custom-call | flops 536870912 | bytes 10485760 | tf_op jit(solution)/shard_map/last/pallas_call | solution.py:518
  (14 shorter events, 0.4 us)
Async XLA Ops:
  0.0 39.5 %collective-permute-start.4 = (bf16[32,256,256]{2,1,0:T(8,128)(2,1)}, bf16[32,256,256]{2,1,0:T(8,128)(2,1)}, u32[]{:S(2)}, u32[]{:S(2)}) collective-permute-start(bf16[32,256,256]{2,1,0:T(8,128)(2,1)} %bitcast.16), channel_id=1, source_target_pairs={{0,2},{2,0},{1,3},{3,1},{4,6},{6,4},{5,7},{7,5},{8,10},{10,8},{9,1... | collective-permute-start | bytes 12582920 | tf_op jit(solution)/shard_map/ppermute | solution.py:573
  16.1 2.1 %collective-permute-start.1 = (bf16[8,256,128]{2,1,0:T(8,128)(2,1)S(1)}, bf16[8,256,128]{2,1,0:T(8,128)(2,1)S(1)}, u32[]{:S(2)}, u32[]{:S(2)}) collective-permute-start(bf16[8,256,128]{2,1,0:T(8,128)(2,1)S(1)} %pick.1.picked), channel_id=1, source_target_pairs={{0,2},{2,0},{1,3},{3,1},{4,6},{6,4},{5,7},{7,5},{8,10},{10,8},{9,1... | collective-permute-start | bytes 1572872 | tf_op jit(solution)/shard_map/ppermute | solution.py:574
  16.8 2.3 %collective-permute-start = (s32[8,128]{1,0:T(8,128)S(1)}, s32[8,128]{1,0:T(8,128)S(1)}, u32[]{:S(2)}, u32[]{:S(2)}) collective-permute-start(s32[8,128]{1,0:T(8,128)S(1)} %bitcast.14), channel_id=1, source_target_pairs={{0,2},{2,0},{1,3},{3,1},{4,6},{6,4},{5,7},{7,5},{8,10},{10,8},{9,1... | collective-permute-start | bytes 12296 | tf_op jit(solution)/shard_map/ppermute | solution.py:575
  18.2 1.1 %collective-permute-start.2 = (s32[65]{0:T(128)S(1)}, s32[65]{0:T(128)S(1)}, u32[]{:S(2)}, u32[]{:S(2)}) collective-permute-start(s32[65]{0:T(128)S(1)} %pad_add_fusion.meta_a), channel_id=1, source_target_pairs={{0,2},{2,0},{1,3},{3,1},{4,6},{6,4},{5,7},{7,5},{8,10},{10,8},{9,1... | collective-permute-start | bytes 788 | tf_op jit(solution)/shard_map/ppermute | solution.py:577
  25.8 13.7 %all-to-all-start.1 = ((bf16[8,256,128]{2,1,0:T(8,128)(2,1)}), bf16[8,256,128]{2,1,0:T(8,128)(2,1)S(1)}, u32[]{:S(2)}, u32[]{:S(2)}) async-start(bf16[8,256,128]{2,1,0:T(8,128)(2,1)} %pack.1.start.previous), calls=%async_computation.1 | async-start | bytes 1048576 | tf_op jit(solution)/shard_map/all_to_all | solution.py:604
  29.3 1.4 %collective-permute-start.3 = (s32[2048]{0:T(1024)}, s32[2048]{0:T(1024)S(1)}, u32[]{:S(2)}, u32[]{:S(2)}) collective-permute-start(s32[2048]{0:T(1024)} %get-tuple-element.28), channel_id=1, source_target_pairs={{0,2},{2,0},{1,3},{3,1},{4,6},{6,4},{5,7},{7,5},{8,10},{10,8},{9,1... | collective-permute-start | bytes 24584 | tf_op jit(solution)/shard_map/ppermute | solution.py:608
  30.8 0.7 copy-start
  59.3 13.7 %all-to-all-start.3 = ((bf16[8,256,128]{2,1,0:T(8,128)(2,1)}), bf16[8,256,128]{2,1,0:T(8,128)(2,1)S(1)}, u32[]{:S(2)}, u32[]{:S(2)}) async-start(bf16[8,256,128]{2,1,0:T(8,128)(2,1)} %sent.3), calls=%async_computation.3 | async-start | bytes 1048576 | tf_op jit(solution)/shard_map/all_to_all | solution.py:731
  62.8 2.9 %collective-permute-start.5 = (bf16[8,256,128]{2,1,0:T(8,128)(2,1)S(1)}, bf16[8,256,128]{2,1,0:T(8,128)(2,1)S(1)}, u32[]{:S(2)}, u32[]{:S(2)}) collective-permute-start(bf16[8,256,128]{2,1,0:T(8,128)(2,1)S(1)} %all-to-all-done.1.pieces.q1), channel_id=1, source_target_pairs={{0,2},{2,0},{1,3},{3,1},{4,6},{6,4},{5,7},{7,5},{8,10},{10,8},{9,1... | collective-permute-start | bytes 1572872 | tf_op jit(solution)/shard_map/ppermute | solution.py:718
  62.9 2.8 %collective-permute-start.6 = (bf16[8,256,128]{2,1,0:T(8,128)(2,1)S(1)}, bf16[8,256,128]{2,1,0:T(8,128)(2,1)S(1)}, u32[]{:S(2)}, u32[]{:S(2)}) collective-permute-start(bf16[8,256,128]{2,1,0:T(8,128)(2,1)S(1)} %all_to_all.24.pieces.q2), channel_id=1, source_target_pairs={{0,2},{2,0},{1,3},{3,1},{4,6},{6,4},{5,7},{7,5},{8,10},{10,8},{9,1... | collective-permute-start | bytes 1572872 | tf_op jit(solution)/shard_map/ppermute | solution.py:719
  73.0 2.0 %collective-permute-start.7 = (bf16[8,256,128]{2,1,0:T(8,128)(2,1)S(1)}, bf16[8,256,128]{2,1,0:T(8,128)(2,1)S(1)}, u32[]{:S(2)}, u32[]{:S(2)}) collective-permute-start(bf16[8,256,128]{2,1,0:T(8,128)(2,1)S(1)} %all-to-all-done.3.mine), channel_id=1, source_target_pairs={{0,2},{2,0},{1,3},{3,1},{4,6},{6,4},{5,7},{7,5},{8,10},{10,8},{9,1... | collective-permute-start | bytes 1572872 | tf_op jit(solution)/shard_map/ppermute | solution.py:732
where the time goes:
time: 79.3 us; the launch traced here: 79.1 us
  Pallas kernels  31 us (39%)
  blocking collectives  25.8 us (33%)
  waiting for transfers between devices  10.4 us (13%)
  starting transfers between devices  8.76 us (11%)
  other arithmetic  1.53 us (2%)
  between operations  0.8 us (1%)
    pallas_call x10, Pallas kernels, call(): pl.pallas_call(kernel, out_shape=[space(shape, dtype) for shape, dtype, s...  31 us
    all_to_all x1, blocking collectives, on_pair(): wanted = exchange(jnp.broadcast_to(needed, (n_row, LANES)))  13.1 us
    all_to_all x1, blocking collectives, on_pair(): q2 = exchange(first_sent)  12.7 us
    all_to_all x1, waiting for transfers between devices, on_pair(): q1 = exchange(after(packed, own_list))  7.37 us
    all_to_all x1, starting transfers between devices, on_pair(): q1 = exchange(after(packed, own_list))  3.51 us
    all_to_all x1, starting transfers between devices, on_pair(): q3 = after(exchange(second_sent), base)  3.5 us
  transfers between devices with their start and end apart: 10, of which 4 were waited for; matrix products, arithmetic and copies ran while one was open for 2% of the time, Pallas kernels for 25%

commit v1 on v0

--- a/solution.py
+++ b/solution.py
@@ -20,6 +20,7 @@
 LANES = 128
 FEW = 4
 MANY = 4
+AHEAD = 8
 HEAD = 8
 STRIDE = 4
 FIRST = 1
@@ -286,6 +287,25 @@
     each_product(plan, base, ends, part, block_of, pieces, use, before=before)
 
 
+def ahead_kernel(lay, plan, tile_a, tile_b, held, sems):
+    for side, tile in enumerate((tile_a, tile_b)):
+        number = jnp.minimum(plan[4 + side] - side * lay.loads, AHEAD)
+
+        @pl.loop(0, number)
+        def _(i):
+            slot = plan[lay.load_at + side * lay.loads + i]
+            at = side * AHEAD + i
+            pltpu.make_async_copy(tile.at[slot], held.at[at], sems.at[at]).start()
+
+    for side in range(2):
+        number = jnp.minimum(plan[4 + side] - side * lay.loads, AHEAD)
+
+        @pl.loop(0, number)
+        def _(i):
+            at = side * AHEAD + i
+            pltpu.make_async_copy(tile_a.at[0], held.at[at], sems.at[at]).wait()
+
+
 def split_sides(pieces, vec):
     middle = vec.shape[-1] // 2
     column = lax.broadcasted_iota(jnp.int32, (1, vec.shape[-1]), 1)
@@ -304,11 +324,25 @@
 
 
 def first_sent_kernel(
-    lay, plan, tile_a, tile_b, pieces, start, out, blocks, vec, total, held, held_sem, sems
+    lay, plan, tile_a, tile_b, early_blocks, pieces, start, out, blocks, vec, total, held, held_sem, sems
 ):
     n_row = out.shape[0]
-    begin, wait = fetches(plan, lay.load_at, 1, 4, lay.loads, (tile_a, tile_b), blocks, sems)
-    begin()
+    for side, tile in enumerate((tile_a, tile_b)):
+        begin, end = side * lay.loads, plan[4 + side]
+
+        @pl.loop(begin, jnp.minimum(end, begin + AHEAD))
+        def _(i):
+            source = early_blocks.at[side * AHEAD + i - begin]
+            pltpu.make_async_copy(source, blocks.at[i], sems.at[i]).start()
+
+        @pl.loop(begin + AHEAD, end)
+        def _(i):
+            source = tile.at[plan[lay.load_at + i]]
+            pltpu.make_async_copy(source, blocks.at[i], sems.at[i]).start()
+
+    def wait(i):
+        pltpu.make_async_copy(tile_a.at[0], blocks.at[i], sems.at[i]).wait()
+
     copy = pltpu.make_async_copy(start, held, held_sem)
     copy.start()
     split_sides(pieces, vec)
@@ -647,7 +681,7 @@
                 ((2 * lay.loads, block_size, block_size), jnp.bfloat16, VMEM),
             ],
             (plan, tile, tile_other, *args),
-            (LIST, FAR, ANYWHERE, HERE, FAR),
+            (LIST, FAR, ANYWHERE, HERE, HERE, FAR),
             sums + [VMEM(sent_shape, jnp.bfloat16), DMA, DMA((2 * lay.loads,))],
             8,
             "sent",
@@ -711,8 +745,17 @@
         )
         return out.reshape(vectors.shape)
 
-    q1 = after(q1, plan)
-    first_sent, blocks = first_blocks(q1, packed)
+    early_blocks = call(
+        functools.partial(ahead_kernel, lay),
+        [((2 * AHEAD, block_size, block_size), jnp.bfloat16, VMEM)],
+        (plan, tile, tile_other),
+        (LIST, FAR, ANYWHERE),
+        [DMA((2 * AHEAD,))],
+        2,
+        "ahead",
+    )[0]
+    q1 = after(q1, early_blocks)
+    first_sent, blocks = first_blocks(early_blocks, q1, packed)
     q2 = exchange(first_sent)
     second_sent = second_blocks(blocks, q2, first_sent, packed)
     q1_other = across(after(q1, second_sent))

time: 79.3 us -> 84.5 us (1.066); the launches traced: 79.1 us -> 85.3 us
  blocking collectives: 25.8 us -> 29.7 us
  Pallas kernels: 31 us -> 31.9 us
    all_to_all x1, blocking collectives: 12.7 us -> 16.6 us  [on_pair(): q2 = exchange(first_sent)]
    all_to_all x1, waiting for transfers between devices: 1.5 us -> 3.8 us  [on_pair(): q3 = after(exchange(second_sent), base)]
    all_to_all x1, waiting for transfers between devices: 7.37 us -> 5.89 us  [on_pair(): q1 = exchange(after(packed, own_list))]
    pallas_call x10 -> x11, Pallas kernels: 31 us -> 31.9 us  [call(): pl.pallas_call(kernel, out_shape=[space(shape, dtype) for shape, dtype, s...]
where the time goes in v1:
time: 84.5 us; the launch traced here: 85.3 us
  Pallas kernels  31.9 us (38%)
  blocking collectives  29.7 us (35%)
  waiting for transfers between devices  11.2 us (13%)
  starting transfers between devices  9.43 us (11%)
  other arithmetic  1.53 us (2%)
    pallas_call x11, Pallas kernels, call(): pl.pallas_call(kernel, out_shape=[space(shape, dtype) for shape, dtype, s...  31.9 us
    all_to_all x1, blocking collectives, on_pair(): q2 = exchange(first_sent)  16.6 us
    all_to_all x1, blocking collectives, on_pair(): wanted = exchange(jnp.broadcast_to(needed, (n_row, LANES)))  13.1 us
    all_to_all x1, waiting for transfers between devices, on_pair(): q1 = exchange(after(packed, own_list))  5.89 us
    all_to_all x1, starting transfers between devices, on_pair(): q3 = after(exchange(second_sent), base)  4.24 us
    all_to_all x1, waiting for transfers between devices, on_pair(): q3 = after(exchange(second_sent), base)  3.8 us
    all_to_all x1, starting transfers between devices, on_pair(): q1 = exchange(after(packed, own_list))  3.51 us
  transfers between devices with their start and end apart: 10, of which 4 were waited for; matrix products, arithmetic and copies ran while one was open for 2% of the time, Pallas kernels for 25%

profile of v1, /device:TPU:0, one launch (start us, length us, event | category | flops | bytes accessed | tf_op | source)
XLA Modules:
  0.0 85.3 jit_solution(12553686918218845427)
XLA Ops:
  0.0 0.5 collective-permute-start.4
  0.5 0.7 and_select_fusion.1
  1.3 13.1 %all_to_all.23 = s32[8,1,128]{2,1,0:T(1,128)S(1)} all-to-all(s32[8,1,128]{2,1,0:T(1,128)S(1)} %broadcast_in_dim.21), channel_id=1, replica_groups=mesh['row'=8,'col'=2,'vec'=2] {'row'}, dimensions={0} | all-to-all | bytes 8192 | tf_op jit(solution)/shard_map/all_to_all | solution.py:596
  14.4 1.7 %pick.1.picked = bf16[8,256,128]{2,1,0:T(8,128)(2,1)S(1)} custom-call(s32[8,128]{1,0:T(8,128)S(1)} %bitcast.13, bf16[8192,128]{1,0:T(8,128)(2,1)} %vectors.2), custom_call_target="tpu_custom_call" | custom-call | tf_op jit(solution)/shard_map/pick/pallas_call | solution.py:552
  16.8 0.6 collective-permute-start
  17.4 0.7 pad_add_fusion.meta_a
  18.2 0.9 %pack.1.start.previous = bf16[8,256,128]{2,1,0:T(8,128)(2,1)} custom-call(bf16[8,256,128]{2,1,0:T(8,128)(2,1)S(1)} %pick.1.picked, bf16[8,256,128]{2,1,0:T(8,128)(2,1)S(1)} %collective-permute-done.1.picked_b), custom_call_target="tpu_custom_call" | custom-call | tf_op jit(solution)/shard_map/pack/pallas_call | solution.py:552
  19.3 6.3 %plan.1 = (s32[2048]{0:T(1024)}, s32[2048]{0:T(1024)}) custom-call(s32[8,128]{1,0:T(8,128)S(1)} %bitcast.15, s32[8,128]{1,0:T(8,128)S(1)} %collective-permute-done.wanted_b, s32[65]{0:T(128)S(1)} %pad_add_fusion.meta_a, s32[65]{0:T(128)S(1)} %collective-permute-done.2.meta_b), custom_call_target="tpu_custom_call" | custom-call | tf_op jit(solution)/shard_map/plan/pallas_call | solution.py:552
  25.6 3.5 %all-to-all-start.1 = ((bf16[8,256,128]{2,1,0:T(8,128)(2,1)}), bf16[8,256,128]{2,1,0:T(8,128)(2,1)S(1)}, u32[]{:S(2)}, u32[]{:S(2)}) async-start(bf16[8,256,128]{2,1,0:T(8,128)(2,1)} %pack.1.start.previous), calls=%async_computation.1 | async-start | bytes 1048576 | tf_op jit(solution)/shard_map/all_to_all | solution.py:638
  29.2 1.4 %collective-permute-done.3.handed = s32[2048]{0:T(1024)S(1)} collective-permute-done((s32[2048]{0:T(1024)}, s32[2048]{0:T(1024)S(1)}, u32[]{:S(2)}, u32[]{:S(2)}) %collective-permute-start.3) | collective-permute-done | bytes 8224 | tf_op jit(solution)/shard_map/ppermute | solution.py:642
  30.5 0.7 copy-done
  31.2 0.7 settle.1.plan
  31.9 1.5 %ahead.1.early_blocks = bf16[16,256,256]{2,1,0:T(8,128)(2,1)S(1)} custom-call(s32[2048]{0:T(1024)S(4)} %settle.1.plan, bf16[32,256,256]{2,1,0:T(8,128)(2,1)} %bitcast.17, bf16[32,256,256]{2,1,0:T(8,128)(2,1)} %collective-permute-done.4.tile_b), custom_call_target="tpu_custom_call" | custom-call | tf_op jit(solution)/shard_map/ahead/pallas_call | solution.py:552
  33.4 5.9 %all-to-all-done.1.pieces.q1 = bf16[8,256,128]{2,1,0:T(8,128)(2,1)S(1)} async-done(((bf16[8,256,128]{2,1,0:T(8,128)(2,1)}), bf16[8,256,128]{2,1,0:T(8,128)(2,1)S(1)}, u32[]{:S(2)}, u32[]{:S(2)}) %all-to-all-start.1) | async-done | bytes 524320 | tf_op jit(solution)/shard_map/all_to_all | solution.py:638
  39.3 3.6 %sent.2 = (bf16[8,256,128]{2,1,0:T(8,128)(2,1)S(1)}, bf16[66,256,256]{2,1,0:T(8,128)(2,1)S(1)}) custom-call(s32[2048]{0:T(1024)S(4)} %settle.1.plan, bf16[32,256,256]{2,1,0:T(8,128)(2,1)} %bitcast.18, bf16[32,256,256]{2,1,0:T(8,128)(2,1)} %collective-permute-done.4.tile_b, bf16[16,256,256]{2,1,0:T(8,128)(2,1)S(1)} %ahead.1.early_blocks, ...), custom_call_target="tpu_custom_call" | custom-call | flops 134217728 | bytes 2621440 | tf_op jit(solution)/shard_map/sent/pallas_call | solution.py:552
  42.9 16.6 %all_to_all.24.pieces.q2 = bf16[8,256,128]{2,1,0:T(8,128)(2,1)S(1)} all-to-all(bf16[8,256,128]{2,1,0:T(8,128)(2,1)S(1)} %get-tuple-element.32.current), channel_id=1, replica_groups=mesh['row'=8,'col'=2,'vec'=2] {'row'}, dimensions={0} | all-to-all | bytes 1048576 | tf_op jit(solution)/shard_map/all_to_all | solution.py:759
  59.5 2.2 %sent.3 = bf16[8,256,128]{2,1,0:T(8,128)(2,1)} custom-call(s32[2048]{0:T(1024)S(4)} %settle.1.plan, bf16[66,256,256]{2,1,0:T(8,128)(2,1)S(1)} %get-tuple-element.31.blocks, bf16[8,256,128]{2,1,0:T(8,128)(2,1)S(1)} %all_to_all.24.pieces.q2, bf16[8,256,128]{2,1,0:T(8,128)(2,1)S(1)} %get-tuple-element.32.current, bf16[8,256,128]{2,1,0:T(8,128)(2,1)} %pack.1.start.previous), custom_call_target="tpu_custom_call" | custom-call | flops 134217728 | bytes 2621440 | tf_op jit(solution)/shard_map/sent/pallas_call | solution.py:552
  61.7 4.2 %all-to-all-start.3 = ((bf16[8,256,128]{2,1,0:T(8,128)(2,1)}), bf16[8,256,128]{2,1,0:T(8,128)(2,1)S(1)}, u32[]{:S(2)}, u32[]{:S(2)}) async-start(bf16[8,256,128]{2,1,0:T(8,128)(2,1)} %sent.3), calls=%async_computation.3 | async-start | bytes 1048576 | tf_op jit(solution)/shard_map/all_to_all | solution.py:774
  66.0 0.5 collective-permute-start.6
  66.5 2.3 %prime.1.start = f32[33,256,256]{2,1,0:T(8,128)S(1)} custom-call(bf16[8192,128]{1,0:T(8,128)(2,1)} %vectors.2), custom_call_target="tpu_custom_call" | custom-call | bytes 18874368 | tf_op jit(solution)/shard_map/prime/pallas_call | solution.py:552
  68.8 6.4 %early.1 = (bf16[32,256,128]{2,1,0:T(8,128)(2,1)}, f32[33,256,256]{2,1,0:T(8,128)S(1)}) custom-call(s32[2048]{0:T(1024)S(4)} %settle.1.plan, bf16[32,256,256]{2,1,0:T(8,128)(2,1)} %bitcast.19, bf16[32,256,256]{2,1,0:T(8,128)(2,1)} %collective-permute-done.4.tile_b, ...), custom_call_target="tpu_custom_call", output_to_operand_aliasing={{1}: (7, {})} | custom-call | flops 1073741824 | bytes 20971520 | tf_op jit(solution)/shard_map/early/pallas_call | solution.py:552
  75.2 3.8 %all-to-all-done.3.mine = bf16[8,256,128]{2,1,0:T(8,128)(2,1)S(1)} async-done(((bf16[8,256,128]{2,1,0:T(8,128)(2,1)}), bf16[8,256,128]{2,1,0:T(8,128)(2,1)S(1)}, u32[]{:S(2)}, u32[]{:S(2)}) %all-to-all-start.3) | async-done | bytes 524320 | tf_op jit(solution)/shard_map/all_to_all | solution.py:774
  79.0 2.0 %load.1 = (bf16[36,256,256]{2,1,0:T(8,128)(2,1)S(1)}, bf16[32,256,128]{2,1,0:T(8,128)(2,1)S(1)}) custom-call(s32[2048]{0:T(1024)S(4)} %settle.1.plan, bf16[32,256,256]{2,1,0:T(8,128)(2,1)} %bitcast.20, bf16[32,256,128]{2,1,0:T(8,128)(2,1)} %get-tuple-element.36.array), custom_call_target="tpu_custom_call" | custom-call | tf_op jit(solution)/shard_map/load/pallas_call | solution.py:552
  81.0 4.3 %last.1 = bf16[32,256,128]{2,1,0:T(8,128)(2,1)} custom-call(s32[2048]{0:T(1024)S(4)} %settle.1.plan, bf16[36,256,256]{2,1,0:T(8,128)(2,1)S(1)} %get-tuple-element.39.blocks, bf16[32,256,256]{2,1,0:T(8,128)(2,1)} %collective-permute-done.4.tile_b, bf16[8,256,128]{2,1,0:T(8,128)(2,1)S(1)} %all-to-all-done.3.mine, ...), custom_call_target="tpu_custom_call" | custom-call | flops 536870912 | bytes 10485760 | tf_op jit(solution)/shard_map/last/pallas_call | solution.py:552
  (15 shorter events, 0.5 us)
Async XLA Ops:
  0.0 31.9 %collective-permute-start.4 = (bf16[32,256,256]{2,1,0:T(8,128)(2,1)}, bf16[32,256,256]{2,1,0:T(8,128)(2,1)}, u32[]{:S(2)}, u32[]{:S(2)}) collective-permute-start(bf16[32,256,256]{2,1,0:T(8,128)(2,1)} %bitcast.16), channel_id=1, source_target_pairs={{0,2},{2,0},{1,3},{3,1},{4,6},{6,4},{5,7},{7,5},{8,10},{10,8},{9,1... | collective-permute-start | bytes 12582920 | tf_op jit(solution)/shard_map/ppermute | solution.py:607
  16.1 2.1 %collective-permute-start.1 = (bf16[8,256,128]{2,1,0:T(8,128)(2,1)S(1)}, bf16[8,256,128]{2,1,0:T(8,128)(2,1)S(1)}, u32[]{:S(2)}, u32[]{:S(2)}) collective-permute-start(bf16[8,256,128]{2,1,0:T(8,128)(2,1)S(1)} %pick.1.picked), channel_id=1, source_target_pairs={{0,2},{2,0},{1,3},{3,1},{4,6},{6,4},{5,7},{7,5},{8,10},{10,8},{9,1... | collective-permute-start | bytes 1572872 | tf_op jit(solution)/shard_map/ppermute | solution.py:608
  16.8 2.3 %collective-permute-start = (s32[8,128]{1,0:T(8,128)S(1)}, s32[8,128]{1,0:T(8,128)S(1)}, u32[]{:S(2)}, u32[]{:S(2)}) collective-permute-start(s32[8,128]{1,0:T(8,128)S(1)} %bitcast.14), channel_id=1, source_target_pairs={{0,2},{2,0},{1,3},{3,1},{4,6},{6,4},{5,7},{7,5},{8,10},{10,8},{9,1... | collective-permute-start | bytes 12296 | tf_op jit(solution)/shard_map/ppermute | solution.py:609
  18.2 1.1 %collective-permute-start.2 = (s32[65]{0:T(128)S(1)}, s32[65]{0:T(128)S(1)}, u32[]{:S(2)}, u32[]{:S(2)}) collective-permute-start(s32[65]{0:T(128)S(1)} %pad_add_fusion.meta_a), channel_id=1, source_target_pairs={{0,2},{2,0},{1,3},{3,1},{4,6},{6,4},{5,7},{7,5},{8,10},{10,8},{9,1... | collective-permute-start | bytes 788 | tf_op jit(solution)/shard_map/ppermute | solution.py:611
  25.6 13.7 %all-to-all-start.1 = ((bf16[8,256,128]{2,1,0:T(8,128)(2,1)}), bf16[8,256,128]{2,1,0:T(8,128)(2,1)S(1)}, u32[]{:S(2)}, u32[]{:S(2)}) async-start(bf16[8,256,128]{2,1,0:T(8,128)(2,1)} %pack.1.start.previous), calls=%async_computation.1 | async-start | bytes 1048576 | tf_op jit(solution)/shard_map/all_to_all | solution.py:638
  29.1 1.4 %collective-permute-start.3 = (s32[2048]{0:T(1024)}, s32[2048]{0:T(1024)S(1)}, u32[]{:S(2)}, u32[]{:S(2)}) collective-permute-start(s32[2048]{0:T(1024)} %get-tuple-element.28), channel_id=1, source_target_pairs={{0,2},{2,0},{1,3},{3,1},{4,6},{6,4},{5,7},{7,5},{8,10},{10,8},{9,1... | collective-permute-start | bytes 24584 | tf_op jit(solution)/shard_map/ppermute | solution.py:642
  30.5 0.7 copy-start
  61.7 17.3 %all-to-all-start.3 = ((bf16[8,256,128]{2,1,0:T(8,128)(2,1)}), bf16[8,256,128]{2,1,0:T(8,128)(2,1)S(1)}, u32[]{:S(2)}, u32[]{:S(2)}) async-start(bf16[8,256,128]{2,1,0:T(8,128)(2,1)} %sent.3), calls=%async_computation.3 | async-start | bytes 1048576 | tf_op jit(solution)/shard_map/all_to_all | solution.py:774
  66.0 2.8 %collective-permute-start.5 = (bf16[8,256,128]{2,1,0:T(8,128)(2,1)S(1)}, bf16[8,256,128]{2,1,0:T(8,128)(2,1)S(1)}, u32[]{:S(2)}, u32[]{:S(2)}) collective-permute-start(bf16[8,256,128]{2,1,0:T(8,128)(2,1)S(1)} %all-to-all-done.1.pieces.q1), channel_id=1, source_target_pairs={{0,2},{2,0},{1,3},{3,1},{4,6},{6,4},{5,7},{7,5},{8,10},{10,8},{9,1... | collective-permute-start | bytes 1572872 | tf_op jit(solution)/shard_map/ppermute | solution.py:761
  66.0 2.8 %collective-permute-start.6 = (bf16[8,256,128]{2,1,0:T(8,128)(2,1)S(1)}, bf16[8,256,128]{2,1,0:T(8,128)(2,1)S(1)}, u32[]{:S(2)}, u32[]{:S(2)}) collective-permute-start(bf16[8,256,128]{2,1,0:T(8,128)(2,1)S(1)} %all_to_all.24.pieces.q2), channel_id=1, source_target_pairs={{0,2},{2,0},{1,3},{3,1},{4,6},{6,4},{5,7},{7,5},{8,10},{10,8},{9,1... | collective-permute-start | bytes 1572872 | tf_op jit(solution)/shard_map/ppermute | solution.py:762
  79.0 2.0 %collective-permute-start.7 = (bf16[8,256,128]{2,1,0:T(8,128)(2,1)S(1)}, bf16[8,256,128]{2,1,0:T(8,128)(2,1)S(1)}, u32[]{:S(2)}, u32[]{:S(2)}) collective-permute-start(bf16[8,256,128]{2,1,0:T(8,128)(2,1)S(1)} %all-to-all-done.3.mine), channel_id=1, source_target_pairs={{0,2},{2,0},{1,3},{3,1},{4,6},{6,4},{5,7},{7,5},{8,10},{10,8},{9,1... | collective-permute-start | bytes 1572872 | tf_op jit(solution)/shard_map/ppermute | solution.py:775

commit v2 on v0

--- a/solution.py
+++ b/solution.py
@@ -70,6 +70,8 @@
     wanted_b,
     meta_a,
     meta_b,
+    used_a,
+    used_b,
     own,
     other,
     out,
@@ -77,21 +79,20 @@
     seen,
     sems,
 ):
-    slot_count = (meta_a.shape[0] - 1) // 2
+    slot_count = meta_a.shape[1] // 2
 
     def put(at, *values):
         for i, value in enumerate(values):
             out[at + i] = value
 
-    def scan(tile, meta):
-        used = meta[2 * slot_count]
+    def scan(tile, meta, used):
 
 
         def step(s, carry):
             ends, sent, load = carry
-            row = meta[s]
-            piece = meta[slot_count + s] // piece_blocks
-            live = s < used
+            row = meta[0, s]
+            piece = meta[0, slot_count + s] // piece_blocks
+            live = s < used[0, 0]
             half = row // piece_blocks
             local = row - half * piece_blocks
             lower = half == 0
@@ -173,8 +174,8 @@
         for half, wanted in enumerate((wanted_a, wanted_b)):
             for k in range(n_row):
                 asked[half * n_row + k] = wanted[k, 0]
-        scan(0, meta_a)
-        scan(1, meta_b)
+        scan(0, meta_a, used_a)
+        scan(1, meta_b, used_b)
         for core in range(2):
             mark(core)
         copies = [
@@ -538,9 +539,7 @@
 def on_pair(vectors, tile_blocks, block_rows, block_cols, counts):
     n_row = lax.axis_size("row")
     tile = tile_blocks[0, 0]
-    slot_rows = block_rows[0, 0]
     slot_cols = block_cols[0, 0]
-    used = counts[0]
     slot_count, block_size, _ = tile.shape
     width = vectors.shape[1]
     piece_blocks = vectors.shape[0] // block_size
@@ -573,8 +572,9 @@
     tile_other = across(tile)
     sent_other = across(sent)
     wanted_other = across(after(wanted, sent))
-    meta = jnp.concatenate([slot_rows, slot_cols, used])
+    meta = jnp.concatenate([block_rows[0], block_cols[0]], axis=1)
     meta_other = across(after(meta, sent))
+    counts_other = across(after(counts, sent))
     packed = call(
         pack_kernel,
         [(sent_shape, jnp.bfloat16, HBM)],
@@ -590,8 +590,8 @@
     own_list, other_list = call(
         functools.partial(plan_kernel, n_row, piece_blocks, lay),
         [(*list_shape, HBM)] * 2,
-        (wanted, after(wanted_other, packed), meta, meta_other),
-        (SCALARS,) * 4,
+        (wanted, after(wanted_other, packed), meta, meta_other, counts, counts_other),
+        (SCALARS,) * 6,
         [
             SMEM((2 * lay.size,), jnp.int32),
             SMEM((2 * n_row,), jnp.int32),

time: 79.3 us -> 83 us (1.047)
  the two profiles are of different devices: /device:TPU:0 before, /device:TPU:1 now
where the time goes in v2:
time: 83 us; the launch traced here: 82.2 us
  Pallas kernels  29.3 us (35%)
  blocking collectives  25 us (30%)
  starting transfers between devices  23.3 us (28%)
  waiting for transfers between devices  1.59 us (2%)
  other arithmetic  1.53 us (2%)
    pallas_call x10, Pallas kernels, call(): pl.pallas_call(kernel, out_shape=[space(shape, dtype) for shape, dtype, s...  29.3 us
    all_to_all x1, blocking collectives, on_pair(): q2 = exchange(first_sent)  12.9 us
    all_to_all x1, blocking collectives, on_pair(): wanted = exchange(jnp.broadcast_to(needed, (n_row, LANES)))  12.1 us
    ppermute x1, starting transfers between devices, on_pair(): q1_other = across(after(q1, second_sent))  7.48 us
    ppermute x1, starting transfers between devices, on_pair(): across(after(other_list, packed))  6.46 us
    all_to_all x1, starting transfers between devices, on_pair(): q1 = exchange(after(packed, own_list))  3.51 us
    all_to_all x1, starting transfers between devices, on_pair(): q3 = after(exchange(second_sent), base)  3.5 us
  transfers between devices with their start and end apart: 11, of which 3 were waited for; matrix products, arithmetic and copies ran while one was open for 2% of the time, Pallas kernels for 21%

profile of v2, /device:TPU:1, one launch (start us, length us, event | category | flops | bytes accessed | tf_op | source)
XLA Modules:
  0.0 82.2 jit_solution(3044085886314206755)
XLA Ops:
  0.1 0.7 and_select_fusion.1
  0.9 12.1 %all_to_all.23 = s32[8,1,128]{2,1,0:T(1,128)S(1)} all-to-all(s32[8,1,128]{2,1,0:T(1,128)S(1)} %broadcast_in_dim.21), channel_id=1, replica_groups=mesh['row'=8,'col'=2,'vec'=2] {'row'}, dimensions={0} | all-to-all | bytes 8192 | tf_op jit(solution)/shard_map/all_to_all | solution.py:561
  13.0 1.7 %pick.1.picked = bf16[8,256,128]{2,1,0:T(8,128)(2,1)S(1)} custom-call(s32[8,128]{1,0:T(8,128)S(1)} %bitcast.20, bf16[8192,128]{1,0:T(8,128)(2,1)} %vectors.2), custom_call_target="tpu_custom_call" | custom-call | tf_op jit(solution)/shard_map/pick/pallas_call | solution.py:519
  14.7 1.5 %collective-permute-start.1 = (bf16[8,256,128]{2,1,0:T(8,128)(2,1)S(1)}, bf16[8,256,128]{2,1,0:T(8,128)(2,1)S(1)}, u32[]{:S(2)}, u32[]{:S(2)}) collective-permute-start(bf16[8,256,128]{2,1,0:T(8,128)(2,1)S(1)} %pick.1.picked), channel_id=1, source_target_pairs={{0,2},{2,0},{1,3},{3,1},{4,6},{6,4},{5,7},{7,5},{8,10},{10,8},{9,1... | collective-permute-start | bytes 1572872 | tf_op jit(solution)/shard_map/ppermute | solution.py:573
  16.3 0.7 pad_add_fusion.meta_a
  17.7 0.5 collective-permute-start.2
  18.3 0.9 %pack.1.start.previous = bf16[8,256,128]{2,1,0:T(8,128)(2,1)} custom-call(bf16[8,256,128]{2,1,0:T(8,128)(2,1)S(1)} %pick.1.picked, bf16[8,256,128]{2,1,0:T(8,128)(2,1)S(1)} %collective-permute-done.1.picked_b), custom_call_target="tpu_custom_call" | custom-call | tf_op jit(solution)/shard_map/pack/pallas_call | solution.py:519
  19.2 0.4 collective-permute-done.3.used_b
  19.6 1.3 %plan.1 = (s32[2048]{0:T(1024)}, s32[2048]{0:T(1024)}) custom-call(s32[8,128]{1,0:T(8,128)S(1)} %bitcast.22, s32[8,128]{1,0:T(8,128)S(1)} %collective-permute-done.wanted_b, s32[1,64]{1,0:T(1,128)S(1)} %pad_add_fusion.meta_a, s32[1,64]{1,0:T(1,128)S(1)} %collective-permute-done.2.meta_b, s32[1,1]{1,0:T(1,128)S(6)} %copy.8.used_a, ...), custom_call_target="tpu_custom_call" | custom-call | tf_op jit(solution)/shard_map/plan/pallas_call | solution.py:519
  20.9 3.5 %all-to-all-start.1 = ((bf16[8,256,128]{2,1,0:T(8,128)(2,1)}), bf16[8,256,128]{2,1,0:T(8,128)(2,1)S(1)}, u32[]{:S(2)}, u32[]{:S(2)}) async-start(bf16[8,256,128]{2,1,0:T(8,128)(2,1)} %pack.1.start.previous), calls=%async_computation.1 | async-start | bytes 1048576 | tf_op jit(solution)/shard_map/all_to_all | solution.py:604
  24.5 6.5 %collective-permute-start.4 = (s32[2048]{0:T(1024)}, s32[2048]{0:T(1024)S(1)}, u32[]{:S(2)}, u32[]{:S(2)}) collective-permute-start(s32[2048]{0:T(1024)} %get-tuple-element.30), channel_id=1, source_target_pairs={{0,2},{2,0},{1,3},{3,1},{4,6},{6,4},{5,7},{7,5},{8,10},{10,8},{9,1... | collective-permute-start | bytes 24584 | tf_op jit(solution)/shard_map/ppermute | solution.py:608
  30.9 1.0 %collective-permute-done.4.handed = s32[2048]{0:T(1024)S(1)} collective-permute-done((s32[2048]{0:T(1024)}, s32[2048]{0:T(1024)S(1)}, u32[]{:S(2)}, u32[]{:S(2)}) %collective-permute-start.4) | collective-permute-done | bytes 8224 | tf_op jit(solution)/shard_map/ppermute | solution.py:608
  32.0 0.7 copy-done
  32.7 0.7 settle.1.plan
  33.3 0.2 all-to-all-done.1.pieces.q1
  33.5 3.7 %sent.2 = (bf16[8,256,128]{2,1,0:T(8,128)(2,1)S(1)}, bf16[66,256,256]{2,1,0:T(8,128)(2,1)S(1)}) custom-call(s32[2048]{0:T(1024)S(4)} %settle.1.plan, bf16[32,256,256]{2,1,0:T(8,128)(2,1)} %bitcast.24, bf16[32,256,256]{2,1,0:T(8,128)(2,1)} %collective-permute-done.5.tile_b, bf16[8,256,128]{2,1,0:T(8,128)(2,1)S(1)} %all-to-all-done.1.pieces.q1, ...), custom_call_target="tpu_custom_call" | custom-call | flops 134217728 | bytes 2621440 | tf_op jit(solution)/shard_map/sent/pallas_call | solution.py:519
  37.2 12.9 %all_to_all.24.pieces.q2 = bf16[8,256,128]{2,1,0:T(8,128)(2,1)S(1)} all-to-all(bf16[8,256,128]{2,1,0:T(8,128)(2,1)S(1)} %get-tuple-element.34.current), channel_id=1, replica_groups=mesh['row'=8,'col'=2,'vec'=2] {'row'}, dimensions={0} | all-to-all | bytes 1048576 | tf_op jit(solution)/shard_map/all_to_all | solution.py:716
  50.1 2.8 %sent.3 = bf16[8,256,128]{2,1,0:T(8,128)(2,1)} custom-call(s32[2048]{0:T(1024)S(4)} %settle.1.plan, bf16[66,256,256]{2,1,0:T(8,128)(2,1)S(1)} %get-tuple-element.33.blocks, bf16[8,256,128]{2,1,0:T(8,128)(2,1)S(1)} %all_to_all.24.pieces.q2, bf16[8,256,128]{2,1,0:T(8,128)(2,1)S(1)} %get-tuple-element.34.current, bf16[8,256,128]{2,1,0:T(8,128)(2,1)} %pack.1.start.previous), custom_call_target="tpu_custom_call" | custom-call | flops 134217728 | bytes 2621440 | tf_op jit(solution)/shard_map/sent/pallas_call | solution.py:519
  52.9 3.5 %all-to-all-start.3 = ((bf16[8,256,128]{2,1,0:T(8,128)(2,1)}), bf16[8,256,128]{2,1,0:T(8,128)(2,1)S(1)}, u32[]{:S(2)}, u32[]{:S(2)}) async-start(bf16[8,256,128]{2,1,0:T(8,128)(2,1)} %sent.3), calls=%async_computation.3 | async-start | bytes 1048576 | tf_op jit(solution)/shard_map/all_to_all | solution.py:731
  56.4 7.5 %collective-permute-start.6 = (bf16[8,256,128]{2,1,0:T(8,128)(2,1)S(1)}, bf16[8,256,128]{2,1,0:T(8,128)(2,1)S(1)}, u32[]{:S(2)}, u32[]{:S(2)}) collective-permute-start(bf16[8,256,128]{2,1,0:T(8,128)(2,1)S(1)} %all-to-all-done.1.pieces.q1), channel_id=1, source_target_pairs={{0,2},{2,0},{1,3},{3,1},{4,6},{6,4},{5,7},{7,5},{8,10},{10,8},{9,1... | collective-permute-start | bytes 1572872 | tf_op jit(solution)/shard_map/ppermute | solution.py:718
  64.0 2.3 %prime.1.start = f32[33,256,256]{2,1,0:T(8,128)S(1)} custom-call(bf16[8192,128]{1,0:T(8,128)(2,1)} %vectors.2), custom_call_target="tpu_custom_call" | custom-call | bytes 18874368 | tf_op jit(solution)/shard_map/prime/pallas_call | solution.py:519
  66.3 7.8 %early.1 = (bf16[32,256,128]{2,1,0:T(8,128)(2,1)}, f32[33,256,256]{2,1,0:T(8,128)S(1)}) custom-call(s32[2048]{0:T(1024)S(4)} %settle.1.plan, bf16[32,256,256]{2,1,0:T(8,128)(2,1)} %bitcast.25, bf16[32,256,256]{2,1,0:T(8,128)(2,1)} %collective-permute-done.5.tile_b, ...), custom_call_target="tpu_custom_call", output_to_operand_aliasing={{1}: (7, {})} | custom-call | flops 1073741824 | bytes 20971520 | tf_op jit(solution)/shard_map/early/pallas_call | solution.py:519
  74.2 2.6 %load.1 = (bf16[36,256,256]{2,1,0:T(8,128)(2,1)S(1)}, bf16[32,256,128]{2,1,0:T(8,128)(2,1)S(1)}) custom-call(s32[2048]{0:T(1024)S(4)} %settle.1.plan, bf16[32,256,256]{2,1,0:T(8,128)(2,1)} %bitcast.26, bf16[32,256,128]{2,1,0:T(8,128)(2,1)} %get-tuple-element.38.array), custom_call_target="tpu_custom_call" | custom-call | tf_op jit(solution)/shard_map/load/pallas_call | solution.py:519
  76.8 5.4 %last.1 = bf16[32,256,128]{2,1,0:T(8,128)(2,1)} custom-call(s32[2048]{0:T(1024)S(4)} %settle.1.plan, bf16[36,256,256]{2,1,0:T(8,128)(2,1)S(1)} %get-tuple-element.41.blocks, bf16[32,256,256]{2,1,0:T(8,128)(2,1)} %collective-permute-done.5.tile_b, bf16[8,256,128]{2,1,0:T(8,128)(2,1)S(1)} %all-to-all-done.3.mine, ...), custom_call_target="tpu_custom_call" | custom-call | flops 536870912 | bytes 10485760 | tf_op jit(solution)/shard_map/last/pallas_call | solution.py:519
  (16 shorter events, 0.6 us)
Async XLA Ops:
  0.0 33.5 %collective-permute-start.5 = (bf16[32,256,256]{2,1,0:T(8,128)(2,1)}, bf16[32,256,256]{2,1,0:T(8,128)(2,1)}, u32[]{:S(2)}, u32[]{:S(2)}) collective-permute-start(bf16[32,256,256]{2,1,0:T(8,128)(2,1)} %bitcast.23), channel_id=1, source_target_pairs={{0,2},{2,0},{1,3},{3,1},{4,6},{6,4},{5,7},{7,5},{8,10},{10,8},{9,1... | collective-permute-start | bytes 12582920 | tf_op jit(solution)/shard_map/ppermute | solution.py:572
  14.7 3.6 %collective-permute-start.1 = (bf16[8,256,128]{2,1,0:T(8,128)(2,1)S(1)}, bf16[8,256,128]{2,1,0:T(8,128)(2,1)S(1)}, u32[]{:S(2)}, u32[]{:S(2)}) collective-permute-start(bf16[8,256,128]{2,1,0:T(8,128)(2,1)S(1)} %pick.1.picked), channel_id=1, source_target_pairs={{0,2},{2,0},{1,3},{3,1},{4,6},{6,4},{5,7},{7,5},{8,10},{10,8},{9,1... | collective-permute-start | bytes 1572872 | tf_op jit(solution)/shard_map/ppermute | solution.py:573
  16.2 3.0 %collective-permute-start = (s32[8,128]{1,0:T(8,128)S(1)}, s32[8,128]{1,0:T(8,128)S(1)}, u32[]{:S(2)}, u32[]{:S(2)}) collective-permute-start(s32[8,128]{1,0:T(8,128)S(1)} %bitcast.21), channel_id=1, source_target_pairs={{0,2},{2,0},{1,3},{3,1},{4,6},{6,4},{5,7},{7,5},{8,10},{10,8},{9,1... | collective-permute-start | bytes 12296 | tf_op jit(solution)/shard_map/ppermute | solution.py:574
  17.7 1.9 %collective-permute-start.2 = (s32[1,64]{1,0:T(1,128)S(1)}, s32[1,64]{1,0:T(1,128)S(1)}, u32[]{:S(2)}, u32[]{:S(2)}) collective-permute-start(s32[1,64]{1,0:T(1,128)S(1)} %pad_add_fusion.meta_a), channel_id=1, source_target_pairs={{0,2},{2,0},{1,3},{3,1},{4,6},{6,4},{5,7},{7,5},{8,10},{10,8},{9,1... | collective-permute-start | bytes 776 | tf_op jit(solution)/shard_map/ppermute | solution.py:576
  18.2 1.4 %collective-permute-start.3 = (s32[1,1]{1,0:T(1,128)}, s32[1,1]{1,0:T(1,128)}, u32[]{:S(2)}, u32[]{:S(2)}) collective-permute-start(s32[1,1]{1,0:T(1,128)} %param.9), channel_id=1, source_target_pairs={{0,2},{2,0},{1,3},{3,1},{4,6},{6,4},{5,7},{7,5},{8,10},{10,8},{9,1... | collective-permute-start | bytes 20 | tf_op jit(solution)/shard_map/ppermute | solution.py:577
  20.9 12.6 %all-to-all-start.1 = ((bf16[8,256,128]{2,1,0:T(8,128)(2,1)}), bf16[8,256,128]{2,1,0:T(8,128)(2,1)S(1)}, u32[]{:S(2)}, u32[]{:S(2)}) async-start(bf16[8,256,128]{2,1,0:T(8,128)(2,1)} %pack.1.start.previous), calls=%async_computation.1 | async-start | bytes 1048576 | tf_op jit(solution)/shard_map/all_to_all | solution.py:604
  24.5 7.5 %collective-permute-start.4 = (s32[2048]{0:T(1024)}, s32[2048]{0:T(1024)S(1)}, u32[]{:S(2)}, u32[]{:S(2)}) collective-permute-start(s32[2048]{0:T(1024)} %get-tuple-element.30), channel_id=1, source_target_pairs={{0,2},{2,0},{1,3},{3,1},{4,6},{6,4},{5,7},{7,5},{8,10},{10,8},{9,1... | collective-permute-start | bytes 24584 | tf_op jit(solution)/shard_map/ppermute | solution.py:608
  32.0 0.7 copy-start
  52.9 21.2 %all-to-all-start.3 = ((bf16[8,256,128]{2,1,0:T(8,128)(2,1)}), bf16[8,256,128]{2,1,0:T(8,128)(2,1)S(1)}, u32[]{:S(2)}, u32[]{:S(2)}) async-start(bf16[8,256,128]{2,1,0:T(8,128)(2,1)} %sent.3), calls=%async_computation.3 | async-start | bytes 1048576 | tf_op jit(solution)/shard_map/all_to_all | solution.py:731
  56.4 9.8 %collective-permute-start.6 = (bf16[8,256,128]{2,1,0:T(8,128)(2,1)S(1)}, bf16[8,256,128]{2,1,0:T(8,128)(2,1)S(1)}, u32[]{:S(2)}, u32[]{:S(2)}) collective-permute-start(bf16[8,256,128]{2,1,0:T(8,128)(2,1)S(1)} %all-to-all-done.1.pieces.q1), channel_id=1, source_target_pairs={{0,2},{2,0},{1,3},{3,1},{4,6},{6,4},{5,7},{7,5},{8,10},{10,8},{9,1... | collective-permute-start | bytes 1572872 | tf_op jit(solution)/shard_map/ppermute | solution.py:718
  63.9 2.4 %collective-permute-start.7 = (bf16[8,256,128]{2,1,0:T(8,128)(2,1)S(1)}, bf16[8,256,128]{2,1,0:T(8,128)(2,1)S(1)}, u32[]{:S(2)}, u32[]{:S(2)}) collective-permute-start(bf16[8,256,128]{2,1,0:T(8,128)(2,1)S(1)} %all_to_all.24.pieces.q2), channel_id=1, source_target_pairs={{0,2},{2,0},{1,3},{3,1},{4,6},{6,4},{5,7},{7,5},{8,10},{10,8},{9,1... | collective-permute-start | bytes 1572872 | tf_op jit(solution)/shard_map/ppermute | solution.py:719
  74.1 2.7 %collective-permute-start.8 = (bf16[8,256,128]{2,1,0:T(8,128)(2,1)S(1)}, bf16[8,256,128]{2,1,0:T(8,128)(2,1)S(1)}, u32[]{:S(2)}, u32[]{:S(2)}) collective-permute-start(bf16[8,256,128]{2,1,0:T(8,128)(2,1)S(1)} %all-to-all-done.3.mine), channel_id=1, source_target_pairs={{0,2},{2,0},{1,3},{3,1},{4,6},{6,4},{5,7},{7,5},{8,10},{10,8},{9,1... | collective-permute-start | bytes 1572872 | tf_op jit(solution)/shard_map/ppermute | solution.py:732

commit v3 on v0

--- a/solution.py
+++ b/solution.py
@@ -20,6 +20,7 @@
 LANES = 128
 FEW = 4
 MANY = 4
+LEAD = 3 * MANY
 HEAD = 8
 STRIDE = 4
 FIRST = 1
@@ -249,29 +250,41 @@
 def load_kernel(plan, tile_a, array, blocks, held, sems, held_sem):
     whole = pltpu.make_async_copy(array, held, held_sem)
     whole.start()
-    start, wait = fetches(plan, HEAD, STRIDE, 0, 0, (tile_a,), blocks, sems)
-    start()
-
-    @pl.loop(0, plan[0])
+    number = jnp.minimum(plan[0], LEAD)
+
+    def copy(i):
+        return pltpu.make_async_copy(
+            tile_a.at[plan[HEAD + STRIDE * i]], blocks.at[i], sems.at[i]
+        )
+
+    @pl.loop(0, number)
     def _(i):
-        wait(i)
+        copy(i).start()
+
+    @pl.loop(0, number)
+    def _(i):
+        copy(i).wait()
 
     whole.wait()
 
 
-def each_product(plan, base, ends, part, block_of, pieces, use, then=None, before=None):
+def each_product(
+    plan, base, ends, part, block_of, pieces, use, then=None, before=None, segments=None
+):
     unroll = MANY if base == HEAD else FEW
 
-    for side in range(2):
-
-        @pl.loop(side * part // unroll, plan[ends + side] // unroll)
+    if segments is None:
+        segments = [(side, side * part, plan[ends + side]) for side in range(2)]
+    for number, (side, begin, end) in enumerate(segments):
+
+        @pl.loop(begin // unroll, end // unroll)
         def _(j):
             step = [(unroll * j + u, base + STRIDE * (unroll * j + u)) for u in range(unroll)]
             if before is not None:
                 for i, entry in step:
-                    before(side, i, entry)
+                    before(number, i, entry)
             for i, entry in step:
-                block = block_of(side, i, entry)
+                block = block_of(number, i, entry)
                 piece = pieces[side][plan[entry + 2]]
                 use(entry, jnp.dot(block, piece, preferred_element_type=jnp.float32))
             if then is not None:
@@ -454,18 +467,24 @@
 
 
 def last_kernel(
-    lay, plan, blocks, tile_b, mine, other, base, out, vec, total, own, blocks_b, sems, row_sems
+    lay, plan, blocks, tile_a, tile_b, mine, other, base, out, vec, total, own, blocks_b, sems, row_sems
 ):
     piece_blocks = base.shape[0]
-    begin = lay.slots
-
-    def fetch(i):
+    begin, own_end = lay.slots, plan[0]
+
+    def fetch(tile, i):
         slot = plan[HEAD + STRIDE * i]
-        return pltpu.make_async_copy(tile_b.at[slot], blocks_b.at[i - begin], sems.at[i - begin])
+        return pltpu.make_async_copy(
+            tile.at[slot], blocks_b.at[i - LEAD], sems.at[i - LEAD]
+        )
+
+    @pl.loop(LEAD, own_end)
+    def _(i):
+        fetch(tile_a, i).start()
 
     @pl.loop(begin, plan[1])
     def _(i):
-        fetch(i).start()
+        fetch(tile_b, i).start()
 
     def put(source, b):
         return pltpu.make_async_copy(source.at[b], out.at[b], row_sems.at[b])
@@ -490,15 +509,29 @@
         def _():
             put(own, plan[entry + 1]).start()
 
-    def block_of(side, i, entry):
-        return blocks[i] if side == 0 else blocks_b[i - begin]
-
-    def before(side, i, entry):
-        if side == 1:
-            fetch(i).wait()
-
+    def block_of(number, i, entry):
+        return blocks[i] if number == 0 else blocks_b[i - LEAD]
+
+    def before(number, i, entry):
+        if number > 0:
+            fetch(tile_a, i).wait()
+
+    segments = [
+        (0, 0, jnp.minimum(own_end, LEAD)),
+        (0, LEAD, own_end),
+        (1, begin, plan[1]),
+    ]
     each_product(
-        plan, HEAD, 0, lay.slots, block_of, (vec.at[0], vec.at[1]), use, then, before
+        plan,
+        HEAD,
+        0,
+        lay.slots,
+        block_of,
+        (vec.at[0], vec.at[1]),
+        use,
+        then,
+        before,
+        segments,
     )
 
     @pl.loop(0, piece_blocks)
@@ -616,12 +649,12 @@
         return call(
             load_kernel,
             [
-                ((lay.slots, block_size, block_size), jnp.bfloat16, VMEM),
+                ((LEAD, block_size, block_size), jnp.bfloat16, VMEM),
                 (array.shape, array.dtype, VMEM),
             ],
             (after(plan, cue), tile, array),
             (LIST, FAR, FAR),
-            [DMA((lay.slots,)), DMA],
+            [DMA((LEAD,)), DMA],
             2,
             "load",
         )
@@ -695,17 +728,17 @@
         (out,) = call(
             functools.partial(last_kernel, lay),
             [(base_shape, jnp.bfloat16, HBM)],
-            (plan, blocks, tile_other, *args),
-            (LIST, HERE, ANYWHERE, HERE, HERE, HERE),
+            (plan, blocks, tile, tile_other, *args),
+            (LIST, HERE, FAR, ANYWHERE, HERE, HERE, HERE),
             [
                 VMEM((2, n_row, block_size, width), jnp.bfloat16),
                 VMEM(rows, jnp.float32),
                 VMEM(rows, jnp.bfloat16),
-                VMEM((lay.slots, block_size, block_size), jnp.bfloat16),
-                DMA((lay.slots,)),
+                VMEM((2 * lay.slots - LEAD, block_size, block_size), jnp.bfloat16),
+                DMA((2 * lay.slots - LEAD,)),
                 DMA((piece_blocks,)),
             ],
-            14,
+            18,
             "last",
             cost(slot_count, piece_blocks),
         )

time: 79.3 us -> 78.7 us (level); the launches traced: 79.1 us -> 77.2 us
  Pallas kernels: 31 us -> 27 us
  blocking collectives: 25.8 us -> 27 us
  waiting for transfers between devices: 10.4 us -> 11.3 us
    pallas_call x10, Pallas kernels: 31 us -> 27 us  [call(): pl.pallas_call(kernel, out_shape=[space(shape, dtype) for shape, dtype, s...]
    all_to_all x1, blocking collectives: 12.7 us -> 13.9 us  [on_pair(): q2 = exchange(first_sent)]
    all_to_all x1, waiting for transfers between devices: 1.5 us -> 2.3 us  [on_pair(): q3 = after(exchange(second_sent), base)]
  transfers between devices with their start and end apart: 10 -> 10, of which waited for: 4 -> 5; matrix products, arithmetic and copies ran while one was open for 2% -> 2% of each run, Pallas kernels for 25% -> 24%
where the time goes in v3:
time: 78.7 us; the launch traced here: 77.2 us
  blocking collectives  27 us (34%)
  Pallas kernels  27 us (34%)
  waiting for transfers between devices  11.3 us (14%)
  starting transfers between devices  8.81 us (11%)
  other arithmetic  1.53 us (2%)
  between operations  0.79 us (1%)
    pallas_call x10, Pallas kernels, call(): pl.pallas_call(kernel, out_shape=[space(shape, dtype) for shape, dtype, s...  27 us
    all_to_all x1, blocking collectives, on_pair(): q2 = exchange(first_sent)  13.9 us
    all_to_all x1, blocking collectives, on_pair(): wanted = exchange(jnp.broadcast_to(needed, (n_row, LANES)))  13.1 us
    all_to_all x1, waiting for transfers between devices, on_pair(): q1 = exchange(after(packed, own_list))  7.37 us
    all_to_all x1, starting transfers between devices, on_pair(): q3 = after(exchange(second_sent), base)  3.6 us
    all_to_all x1, starting transfers between devices, on_pair(): q1 = exchange(after(packed, own_list))  3.51 us
    all_to_all x1, waiting for transfers between devices, on_pair(): q3 = after(exchange(second_sent), base)  2.3 us
  transfers between devices with their start and end apart: 10, of which 5 were waited for; matrix products, arithmetic and copies ran while one was open for 2% of the time, Pallas kernels for 24%

profile of v3, /device:TPU:0, one launch (start us, length us, event | category | flops | bytes accessed | tf_op | source)
XLA Modules:
  0.0 77.2 jit_solution(15042962809766019127)
XLA Ops:
  0.0 0.5 collective-permute-start.4
  0.5 0.7 and_select_fusion.1
  1.3 13.1 %all_to_all.23 = s32[8,1,128]{2,1,0:T(1,128)S(1)} all-to-all(s32[8,1,128]{2,1,0:T(1,128)S(1)} %broadcast_in_dim.21), channel_id=1, replica_groups=mesh['row'=8,'col'=2,'vec'=2] {'row'}, dimensions={0} | all-to-all | bytes 8192 | tf_op jit(solution)/shard_map/all_to_all | solution.py:595
  14.4 1.7 %pick.1.picked = bf16[8,256,128]{2,1,0:T(8,128)(2,1)S(1)} custom-call(s32[8,128]{1,0:T(8,128)S(1)} %bitcast.13, bf16[8192,128]{1,0:T(8,128)(2,1)} %vectors.2), custom_call_target="tpu_custom_call" | custom-call | tf_op jit(solution)/shard_map/pick/pallas_call | solution.py:551
  16.8 0.6 collective-permute-start
  17.4 0.7 pad_add_fusion.meta_a
  18.2 0.9 %pack.1.start.previous = bf16[8,256,128]{2,1,0:T(8,128)(2,1)} custom-call(bf16[8,256,128]{2,1,0:T(8,128)(2,1)S(1)} %pick.1.picked, bf16[8,256,128]{2,1,0:T(8,128)(2,1)S(1)} %collective-permute-done.1.picked_b), custom_call_target="tpu_custom_call" | custom-call | tf_op jit(solution)/shard_map/pack/pallas_call | solution.py:551
  19.1 0.1 collective-permute-done.2.meta_b
  19.3 6.0 %plan.1 = (s32[2048]{0:T(1024)}, s32[2048]{0:T(1024)}) custom-call(s32[8,128]{1,0:T(8,128)S(1)} %bitcast.15, s32[8,128]{1,0:T(8,128)S(1)} %collective-permute-done.wanted_b, s32[65]{0:T(128)S(1)} %pad_add_fusion.meta_a, s32[65]{0:T(128)S(1)} %collective-permute-done.2.meta_b), custom_call_target="tpu_custom_call" | custom-call | tf_op jit(solution)/shard_map/plan/pallas_call | solution.py:551
  25.3 3.5 %all-to-all-start.1 = ((bf16[8,256,128]{2,1,0:T(8,128)(2,1)}), bf16[8,256,128]{2,1,0:T(8,128)(2,1)S(1)}, u32[]{:S(2)}, u32[]{:S(2)}) async-start(bf16[8,256,128]{2,1,0:T(8,128)(2,1)} %pack.1.start.previous), calls=%async_computation.1 | async-start | bytes 1048576 | tf_op jit(solution)/shard_map/all_to_all | solution.py:637
  28.8 1.4 %collective-permute-done.3.handed = s32[2048]{0:T(1024)S(1)} collective-permute-done((s32[2048]{0:T(1024)}, s32[2048]{0:T(1024)S(1)}, u32[]{:S(2)}, u32[]{:S(2)}) %collective-permute-start.3) | collective-permute-done | bytes 8224 | tf_op jit(solution)/shard_map/ppermute | solution.py:641
  30.2 0.7 copy-done
  30.9 0.7 settle.1.plan
  31.6 7.4 %all-to-all-done.1.pieces.q1 = bf16[8,256,128]{2,1,0:T(8,128)(2,1)S(1)} async-done(((bf16[8,256,128]{2,1,0:T(8,128)(2,1)}), bf16[8,256,128]{2,1,0:T(8,128)(2,1)S(1)}, u32[]{:S(2)}, u32[]{:S(2)}) %all-to-all-start.1) | async-done | bytes 524320 | tf_op jit(solution)/shard_map/all_to_all | solution.py:637
  39.0 2.5 %sent.2 = (bf16[8,256,128]{2,1,0:T(8,128)(2,1)S(1)}, bf16[66,256,256]{2,1,0:T(8,128)(2,1)S(1)}) custom-call(s32[2048]{0:T(1024)S(4)} %settle.1.plan, bf16[32,256,256]{2,1,0:T(8,128)(2,1)} %bitcast.17, bf16[32,256,256]{2,1,0:T(8,128)(2,1)} %collective-permute-done.4.tile_b, bf16[8,256,128]{2,1,0:T(8,128)(2,1)S(1)} %all-to-all-done.1.pieces.q1, ...), custom_call_target="tpu_custom_call" | custom-call | flops 134217728 | bytes 2621440 | tf_op jit(solution)/shard_map/sent/pallas_call | solution.py:551
  41.5 13.9 %all_to_all.24.pieces.q2 = bf16[8,256,128]{2,1,0:T(8,128)(2,1)S(1)} all-to-all(bf16[8,256,128]{2,1,0:T(8,128)(2,1)S(1)} %get-tuple-element.32.current), channel_id=1, replica_groups=mesh['row'=8,'col'=2,'vec'=2] {'row'}, dimensions={0} | all-to-all | bytes 1048576 | tf_op jit(solution)/shard_map/all_to_all | solution.py:749
  55.4 2.1 %sent.3 = bf16[8,256,128]{2,1,0:T(8,128)(2,1)} custom-call(s32[2048]{0:T(1024)S(4)} %settle.1.plan, bf16[66,256,256]{2,1,0:T(8,128)(2,1)S(1)} %get-tuple-element.31.blocks, bf16[8,256,128]{2,1,0:T(8,128)(2,1)S(1)} %all_to_all.24.pieces.q2, bf16[8,256,128]{2,1,0:T(8,128)(2,1)S(1)} %get-tuple-element.32.current, bf16[8,256,128]{2,1,0:T(8,128)(2,1)} %pack.1.start.previous), custom_call_target="tpu_custom_call" | custom-call | flops 134217728 | bytes 2621440 | tf_op jit(solution)/shard_map/sent/pallas_call | solution.py:551
  57.5 3.6 %all-to-all-start.3 = ((bf16[8,256,128]{2,1,0:T(8,128)(2,1)}), bf16[8,256,128]{2,1,0:T(8,128)(2,1)S(1)}, u32[]{:S(2)}, u32[]{:S(2)}) async-start(bf16[8,256,128]{2,1,0:T(8,128)(2,1)} %sent.3), calls=%async_computation.3 | async-start | bytes 1048576 | tf_op jit(solution)/shard_map/all_to_all | solution.py:764
  61.2 0.5 collective-permute-start.6
  61.7 2.3 %prime.1.start = f32[33,256,256]{2,1,0:T(8,128)S(1)} custom-call(bf16[8192,128]{1,0:T(8,128)(2,1)} %vectors.2), custom_call_target="tpu_custom_call" | custom-call | bytes 18874368 | tf_op jit(solution)/shard_map/prime/pallas_call | solution.py:551
  64.0 5.1 %early.1 = (bf16[32,256,128]{2,1,0:T(8,128)(2,1)}, f32[33,256,256]{2,1,0:T(8,128)S(1)}) custom-call(s32[2048]{0:T(1024)S(4)} %settle.1.plan, bf16[32,256,256]{2,1,0:T(8,128)(2,1)} %bitcast.18, bf16[32,256,256]{2,1,0:T(8,128)(2,1)} %collective-permute-done.4.tile_b, ...), custom_call_target="tpu_custom_call", output_to_operand_aliasing={{1}: (7, {})} | custom-call | flops 1073741824 | bytes 20971520 | tf_op jit(solution)/shard_map/early/pallas_call | solution.py:551
  69.1 2.3 %all-to-all-done.3.mine = bf16[8,256,128]{2,1,0:T(8,128)(2,1)S(1)} async-done(((bf16[8,256,128]{2,1,0:T(8,128)(2,1)}), bf16[8,256,128]{2,1,0:T(8,128)(2,1)S(1)}, u32[]{:S(2)}, u32[]{:S(2)}) %all-to-all-start.3) | async-done | bytes 524320 | tf_op jit(solution)/shard_map/all_to_all | solution.py:764
  71.4 1.8 %load.1 = (bf16[12,256,256]{2,1,0:T(8,128)(2,1)S(1)}, bf16[32,256,128]{2,1,0:T(8,128)(2,1)S(1)}) custom-call(s32[2048]{0:T(1024)S(4)} %settle.1.plan, bf16[32,256,256]{2,1,0:T(8,128)(2,1)} %bitcast.19, bf16[32,256,128]{2,1,0:T(8,128)(2,1)} %get-tuple-element.36.array), custom_call_target="tpu_custom_call" | custom-call | tf_op jit(solution)/shard_map/load/pallas_call | solution.py:551
  73.3 3.9 %last.1 = bf16[32,256,128]{2,1,0:T(8,128)(2,1)} custom-call(s32[2048]{0:T(1024)S(4)} %settle.1.plan, bf16[12,256,256]{2,1,0:T(8,128)(2,1)S(1)} %get-tuple-element.39.blocks, bf16[32,256,256]{2,1,0:T(8,128)(2,1)} %bitcast.20, bf16[32,256,256]{2,1,0:T(8,128)(2,1)} %collective-permute-done.4.tile_b, bf16[8,256,128]{2,1,0:T(8,128)(2,1)S(1)} %all-to-all-done.3.mine, ...), custom_call_target="tpu_custom_call" | custom-call | flops 536870912 | bytes 10485760 | tf_op jit(solution)/shard_map/last/pallas_call | solution.py:551
  (14 shorter events, 0.5 us)
Async XLA Ops:
  0.0 39.0 %collective-permute-start.4 = (bf16[32,256,256]{2,1,0:T(8,128)(2,1)}, bf16[32,256,256]{2,1,0:T(8,128)(2,1)}, u32[]{:S(2)}, u32[]{:S(2)}) collective-permute-start(bf16[32,256,256]{2,1,0:T(8,128)(2,1)} %bitcast.16), channel_id=1, source_target_pairs={{0,2},{2,0},{1,3},{3,1},{4,6},{6,4},{5,7},{7,5},{8,10},{10,8},{9,1... | collective-permute-start | bytes 12582920 | tf_op jit(solution)/shard_map/ppermute | solution.py:606
  16.1 2.1 %collective-permute-start.1 = (bf16[8,256,128]{2,1,0:T(8,128)(2,1)S(1)}, bf16[8,256,128]{2,1,0:T(8,128)(2,1)S(1)}, u32[]{:S(2)}, u32[]{:S(2)}) collective-permute-start(bf16[8,256,128]{2,1,0:T(8,128)(2,1)S(1)} %pick.1.picked), channel_id=1, source_target_pairs={{0,2},{2,0},{1,3},{3,1},{4,6},{6,4},{5,7},{7,5},{8,10},{10,8},{9,1... | collective-permute-start | bytes 1572872 | tf_op jit(solution)/shard_map/ppermute | solution.py:607
  16.8 2.3 %collective-permute-start = (s32[8,128]{1,0:T(8,128)S(1)}, s32[8,128]{1,0:T(8,128)S(1)}, u32[]{:S(2)}, u32[]{:S(2)}) collective-permute-start(s32[8,128]{1,0:T(8,128)S(1)} %bitcast.14), channel_id=1, source_target_pairs={{0,2},{2,0},{1,3},{3,1},{4,6},{6,4},{5,7},{7,5},{8,10},{10,8},{9,1... | collective-permute-start | bytes 12296 | tf_op jit(solution)/shard_map/ppermute | solution.py:608
  18.2 1.1 %collective-permute-start.2 = (s32[65]{0:T(128)S(1)}, s32[65]{0:T(128)S(1)}, u32[]{:S(2)}, u32[]{:S(2)}) collective-permute-start(s32[65]{0:T(128)S(1)} %pad_add_fusion.meta_a), channel_id=1, source_target_pairs={{0,2},{2,0},{1,3},{3,1},{4,6},{6,4},{5,7},{7,5},{8,10},{10,8},{9,1... | collective-permute-start | bytes 788 | tf_op jit(solution)/shard_map/ppermute | solution.py:610
  25.3 13.7 %all-to-all-start.1 = ((bf16[8,256,128]{2,1,0:T(8,128)(2,1)}), bf16[8,256,128]{2,1,0:T(8,128)(2,1)S(1)}, u32[]{:S(2)}, u32[]{:S(2)}) async-start(bf16[8,256,128]{2,1,0:T(8,128)(2,1)} %pack.1.start.previous), calls=%async_computation.1 | async-start | bytes 1048576 | tf_op jit(solution)/shard_map/all_to_all | solution.py:637
  28.8 1.4 %collective-permute-start.3 = (s32[2048]{0:T(1024)}, s32[2048]{0:T(1024)S(1)}, u32[]{:S(2)}, u32[]{:S(2)}) collective-permute-start(s32[2048]{0:T(1024)} %get-tuple-element.28), channel_id=1, source_target_pairs={{0,2},{2,0},{1,3},{3,1},{4,6},{6,4},{5,7},{7,5},{8,10},{10,8},{9,1... | collective-permute-start | bytes 24584 | tf_op jit(solution)/shard_map/ppermute | solution.py:641
  30.2 0.7 copy-start
  57.5 13.9 %all-to-all-start.3 = ((bf16[8,256,128]{2,1,0:T(8,128)(2,1)}), bf16[8,256,128]{2,1,0:T(8,128)(2,1)S(1)}, u32[]{:S(2)}, u32[]{:S(2)}) async-start(bf16[8,256,128]{2,1,0:T(8,128)(2,1)} %sent.3), calls=%async_computation.3 | async-start | bytes 1048576 | tf_op jit(solution)/shard_map/all_to_all | solution.py:764
  61.1 2.8 %collective-permute-start.5 = (bf16[8,256,128]{2,1,0:T(8,128)(2,1)S(1)}, bf16[8,256,128]{2,1,0:T(8,128)(2,1)S(1)}, u32[]{:S(2)}, u32[]{:S(2)}) collective-permute-start(bf16[8,256,128]{2,1,0:T(8,128)(2,1)S(1)} %all-to-all-done.1.pieces.q1), channel_id=1, source_target_pairs={{0,2},{2,0},{1,3},{3,1},{4,6},{6,4},{5,7},{7,5},{8,10},{10,8},{9,1... | collective-permute-start | bytes 1572872 | tf_op jit(solution)/shard_map/ppermute | solution.py:751
  61.2 2.8 %collective-permute-start.6 = (bf16[8,256,128]{2,1,0:T(8,128)(2,1)S(1)}, bf16[8,256,128]{2,1,0:T(8,128)(2,1)S(1)}, u32[]{:S(2)}, u32[]{:S(2)}) collective-permute-start(bf16[8,256,128]{2,1,0:T(8,128)(2,1)S(1)} %all_to_all.24.pieces.q2), channel_id=1, source_target_pairs={{0,2},{2,0},{1,3},{3,1},{4,6},{6,4},{5,7},{7,5},{8,10},{10,8},{9,1... | collective-permute-start | bytes 1572872 | tf_op jit(solution)/shard_map/ppermute | solution.py:752
  71.4 1.9 %collective-permute-start.7 = (bf16[8,256,128]{2,1,0:T(8,128)(2,1)S(1)}, bf16[8,256,128]{2,1,0:T(8,128)(2,1)S(1)}, u32[]{:S(2)}, u32[]{:S(2)}) collective-permute-start(bf16[8,256,128]{2,1,0:T(8,128)(2,1)S(1)} %all-to-all-done.3.mine), channel_id=1, source_target_pairs={{0,2},{2,0},{1,3},{3,1},{4,6},{6,4},{5,7},{7,5},{8,10},{10,8},{9,1... | collective-permute-start | bytes 1572872 | tf_op jit(solution)/shard_map/ppermute | solution.py:765

commit v4 on v3

--- a/solution.py
+++ b/solution.py
@@ -209,12 +209,12 @@
         fetch(k).wait()
 
 
-def pack_kernel(picked, picked_b, out, held, sems):
+def pack_kernel(picked, picked_b, out, held, sem):
     n_row, _, width = picked.shape
     middle = width // 2
 
     def put(k):
-        return pltpu.make_async_copy(held.at[k], out.at[k], sems.at[k])
+        return pltpu.make_async_copy(held.at[k], out.at[k], sem)
 
     for half in range(2):
 
@@ -225,8 +225,7 @@
                 held[k] = jnp.concatenate([picked[k, :, part], picked_b[k, :, part]], axis=1)
                 put(k).start()
 
-    for k in range(n_row):
-        put(k).wait()
+    pltpu.make_async_copy(held, out, sem).wait()
 
 
 def fetches(plan, base, stride, ends, part, tiles, blocks, sems):
@@ -349,7 +348,7 @@
 
 
 def second_sent_kernel(
-    lay, plan, blocks, pieces, current, previous, out, vec, total, held, held_sem, ready, out_sems
+    lay, plan, blocks, pieces, current, previous, out, vec, total, held, held_sem, ready, out_sem
 ):
     n_row = out.shape[0]
     copy = pltpu.make_async_copy(previous, held, held_sem)
@@ -368,14 +367,13 @@
     copy.wait()
 
     def put(k):
-        return pltpu.make_async_copy(ready.at[k], out.at[k], out_sems.at[k])
+        return pltpu.make_async_copy(ready.at[k], out.at[k], out_sem)
 
     for k in range(n_row):
         value = joined(total, k) - center_value * current[k].astype(jnp.float32)
         ready[k] = (value - held[k].astype(jnp.float32)).astype(jnp.bfloat16)
         put(k).start()
-    for k in range(n_row):
-        put(k).wait()
+    pltpu.make_async_copy(ready, out, out_sem).wait()
 
 
 def whole_columns(half, mine, other, vec, at):
@@ -467,7 +465,7 @@
 
 
 def last_kernel(
-    lay, plan, blocks, tile_a, tile_b, mine, other, base, out, vec, total, own, blocks_b, sems, row_sems
+    lay, plan, blocks, tile_a, tile_b, mine, other, base, out, vec, total, own, blocks_b, sems, out_sem
 ):
     piece_blocks = base.shape[0]
     begin, own_end = lay.slots, plan[0]
@@ -487,7 +485,7 @@
         fetch(tile_b, i).start()
 
     def put(source, b):
-        return pltpu.make_async_copy(source.at[b], out.at[b], row_sems.at[b])
+        return pltpu.make_async_copy(source.at[b], out.at[b], out_sem)
 
     @pl.loop(0, plan[6])
     def _(i):
@@ -534,9 +532,7 @@
         segments,
     )
 
-    @pl.loop(0, piece_blocks)
-    def _(b):
-        put(own, b).wait()
+    pltpu.make_async_copy(base, out, out_sem).wait()
 
 
 def after(value, *others):
@@ -613,7 +609,7 @@
         [(sent_shape, jnp.bfloat16, HBM)],
         (sent, sent_other),
         (HERE, HERE),
-        [VMEM(sent_shape, jnp.bfloat16), DMA((n_row,))],
+        [VMEM(sent_shape, jnp.bfloat16), DMA],
         4,
         "pack",
     )[0]
@@ -694,7 +690,7 @@
             (plan, *args),
             (LIST, HERE, HERE, HERE, FAR),
             sums
-            + [VMEM(sent_shape, jnp.bfloat16), DMA, VMEM(sent_shape, jnp.bfloat16), DMA((n_row,))],
+            + [VMEM(sent_shape, jnp.bfloat16), DMA, VMEM(sent_shape, jnp.bfloat16), DMA],
             8,
             "sent",
             cost(n_row, n_row),
@@ -736,7 +732,7 @@
                 VMEM(rows, jnp.bfloat16),
                 VMEM((2 * lay.slots - LEAD, block_size, block_size), jnp.bfloat16),
                 DMA((2 * lay.slots - LEAD,)),
-                DMA((piece_blocks,)),
+                DMA,
             ],
             18,
             "last",

time: 78.7 us -> 78.2 us (level); the launches traced: 77.2 us -> 77.9 us
  Pallas kernels: 27 us -> 25.1 us
  blocking collectives: 27 us -> 28.6 us
    pallas_call x10, Pallas kernels: 27 us -> 25.1 us  [call(): pl.pallas_call(kernel, out_shape=[space(shape, dtype) for shape, dtype, s...]
    all_to_all x1, blocking collectives: 13.9 us -> 15.5 us  [on_pair(): q2 = exchange(first_sent)]
  transfers between devices with their start and end apart: 10 -> 10, of which waited for: 5 -> 5; matrix products, arithmetic and copies ran while one was open for 2% -> 2% of each run, Pallas kernels for 24% -> 23%
where the time goes in v4:
time: 78.2 us; the launch traced here: 77.9 us
  blocking collectives  28.6 us (37%)
  Pallas kernels  25.1 us (32%)
  waiting for transfers between devices  11.7 us (15%)
  starting transfers between devices  9.5 us (12%)
  other arithmetic  1.53 us (2%)
  between operations  0.79 us (1%)
    pallas_call x10, Pallas kernels, call(): pl.pallas_call(kernel, out_shape=[space(shape, dtype) for shape, dtype, s...  25.1 us
    all_to_all x1, blocking collectives, on_pair(): q2 = exchange(first_sent)  15.5 us
    all_to_all x1, blocking collectives, on_pair(): wanted = exchange(jnp.broadcast_to(needed, (n_row, LANES)))  13.1 us
    all_to_all x1, waiting for transfers between devices, on_pair(): q1 = exchange(after(packed, own_list))  7.38 us
    all_to_all x1, starting transfers between devices, on_pair(): q3 = after(exchange(second_sent), base)  4.31 us
    all_to_all x1, starting transfers between devices, on_pair(): q1 = exchange(after(packed, own_list))  3.51 us
    all_to_all x1, waiting for transfers between devices, on_pair(): q3 = after(exchange(second_sent), base)  2.58 us
  transfers between devices with their start and end apart: 10, of which 5 were waited for; matrix products, arithmetic and copies ran while one was open for 2% of the time, Pallas kernels for 23%

profile of v4, /device:TPU:0, one launch (start us, length us, event | category | flops | bytes accessed | tf_op | source)
XLA Modules:
  0.0 77.9 jit_solution(4328661689573448880)
XLA Ops:
  0.0 0.5 collective-permute-start.4
  0.5 0.7 and_select_fusion.1
  1.3 13.1 %all_to_all.23 = s32[8,1,128]{2,1,0:T(1,128)S(1)} all-to-all(s32[8,1,128]{2,1,0:T(1,128)S(1)} %broadcast_in_dim.21), channel_id=1, replica_groups=mesh['row'=8,'col'=2,'vec'=2] {'row'}, dimensions={0} | all-to-all | bytes 8192 | tf_op jit(solution)/shard_map/all_to_all | solution.py:591
  14.4 1.7 %pick.1.picked = bf16[8,256,128]{2,1,0:T(8,128)(2,1)S(1)} custom-call(s32[8,128]{1,0:T(8,128)S(1)} %bitcast.13, bf16[8192,128]{1,0:T(8,128)(2,1)} %vectors.2), custom_call_target="tpu_custom_call" | custom-call | tf_op jit(solution)/shard_map/pick/pallas_call | solution.py:547
  16.8 0.6 collective-permute-start
  17.4 0.7 pad_add_fusion.meta_a
  18.2 0.9 %pack.1.start.previous = bf16[8,256,128]{2,1,0:T(8,128)(2,1)} custom-call(bf16[8,256,128]{2,1,0:T(8,128)(2,1)S(1)} %pick.1.picked, bf16[8,256,128]{2,1,0:T(8,128)(2,1)S(1)} %collective-permute-done.1.picked_b), custom_call_target="tpu_custom_call" | custom-call | tf_op jit(solution)/shard_map/pack/pallas_call | solution.py:547
  19.1 0.2 collective-permute-done.2.meta_b
  19.3 5.6 %plan.1 = (s32[2048]{0:T(1024)}, s32[2048]{0:T(1024)}) custom-call(s32[8,128]{1,0:T(8,128)S(1)} %bitcast.15, s32[8,128]{1,0:T(8,128)S(1)} %collective-permute-done.wanted_b, s32[65]{0:T(128)S(1)} %pad_add_fusion.meta_a, s32[65]{0:T(128)S(1)} %collective-permute-done.2.meta_b), custom_call_target="tpu_custom_call" | custom-call | tf_op jit(solution)/shard_map/plan/pallas_call | solution.py:547
  24.9 3.5 %all-to-all-start.1 = ((bf16[8,256,128]{2,1,0:T(8,128)(2,1)}), bf16[8,256,128]{2,1,0:T(8,128)(2,1)S(1)}, u32[]{:S(2)}, u32[]{:S(2)}) async-start(bf16[8,256,128]{2,1,0:T(8,128)(2,1)} %pack.1.start.previous), calls=%async_computation.1 | async-start | bytes 1048576 | tf_op jit(solution)/shard_map/all_to_all | solution.py:633
  28.5 1.4 %collective-permute-done.3.handed = s32[2048]{0:T(1024)S(1)} collective-permute-done((s32[2048]{0:T(1024)}, s32[2048]{0:T(1024)S(1)}, u32[]{:S(2)}, u32[]{:S(2)}) %collective-permute-start.3) | collective-permute-done | bytes 8224 | tf_op jit(solution)/shard_map/ppermute | solution.py:637
  29.9 0.7 copy-done
  30.6 0.7 settle.1.plan
  31.3 7.4 %all-to-all-done.1.pieces.q1 = bf16[8,256,128]{2,1,0:T(8,128)(2,1)S(1)} async-done(((bf16[8,256,128]{2,1,0:T(8,128)(2,1)}), bf16[8,256,128]{2,1,0:T(8,128)(2,1)S(1)}, u32[]{:S(2)}, u32[]{:S(2)}) %all-to-all-start.1) | async-done | bytes 524320 | tf_op jit(solution)/shard_map/all_to_all | solution.py:633
  38.7 2.0 %sent.2 = (bf16[8,256,128]{2,1,0:T(8,128)(2,1)S(1)}, bf16[66,256,256]{2,1,0:T(8,128)(2,1)S(1)}) custom-call(s32[2048]{0:T(1024)S(4)} %settle.1.plan, bf16[32,256,256]{2,1,0:T(8,128)(2,1)} %bitcast.17, bf16[32,256,256]{2,1,0:T(8,128)(2,1)} %collective-permute-done.4.tile_b, bf16[8,256,128]{2,1,0:T(8,128)(2,1)S(1)} %all-to-all-done.1.pieces.q1, ...), custom_call_target="tpu_custom_call" | custom-call | flops 134217728 | bytes 2621440 | tf_op jit(solution)/shard_map/sent/pallas_call | solution.py:547
  40.7 15.5 %all_to_all.24.pieces.q2 = bf16[8,256,128]{2,1,0:T(8,128)(2,1)S(1)} all-to-all(bf16[8,256,128]{2,1,0:T(8,128)(2,1)S(1)} %get-tuple-element.32.current), channel_id=1, replica_groups=mesh['row'=8,'col'=2,'vec'=2] {'row'}, dimensions={0} | all-to-all | bytes 1048576 | tf_op jit(solution)/shard_map/all_to_all | solution.py:745
  56.1 2.0 %sent.3 = bf16[8,256,128]{2,1,0:T(8,128)(2,1)} custom-call(s32[2048]{0:T(1024)S(4)} %settle.1.plan, bf16[66,256,256]{2,1,0:T(8,128)(2,1)S(1)} %get-tuple-element.31.blocks, bf16[8,256,128]{2,1,0:T(8,128)(2,1)S(1)} %all_to_all.24.pieces.q2, bf16[8,256,128]{2,1,0:T(8,128)(2,1)S(1)} %get-tuple-element.32.current, bf16[8,256,128]{2,1,0:T(8,128)(2,1)} %pack.1.start.previous), custom_call_target="tpu_custom_call" | custom-call | flops 134217728 | bytes 2621440 | tf_op jit(solution)/shard_map/sent/pallas_call | solution.py:547
  58.2 4.3 %all-to-all-start.3 = ((bf16[8,256,128]{2,1,0:T(8,128)(2,1)}), bf16[8,256,128]{2,1,0:T(8,128)(2,1)S(1)}, u32[]{:S(2)}, u32[]{:S(2)}) async-start(bf16[8,256,128]{2,1,0:T(8,128)(2,1)} %sent.3), calls=%async_computation.3 | async-start | bytes 1048576 | tf_op jit(solution)/shard_map/all_to_all | solution.py:760
  62.5 0.5 collective-permute-start.6
  63.0 2.3 %prime.1.start = f32[33,256,256]{2,1,0:T(8,128)S(1)} custom-call(bf16[8192,128]{1,0:T(8,128)(2,1)} %vectors.2), custom_call_target="tpu_custom_call" | custom-call | bytes 18874368 | tf_op jit(solution)/shard_map/prime/pallas_call | solution.py:547
  65.3 4.9 %early.1 = (bf16[32,256,128]{2,1,0:T(8,128)(2,1)}, f32[33,256,256]{2,1,0:T(8,128)S(1)}) custom-call(s32[2048]{0:T(1024)S(4)} %settle.1.plan, bf16[32,256,256]{2,1,0:T(8,128)(2,1)} %bitcast.18, bf16[32,256,256]{2,1,0:T(8,128)(2,1)} %collective-permute-done.4.tile_b, ...), custom_call_target="tpu_custom_call", output_to_operand_aliasing={{1}: (7, {})} | custom-call | flops 1073741824 | bytes 20971520 | tf_op jit(solution)/shard_map/early/pallas_call | solution.py:547
  70.2 2.6 %all-to-all-done.3.mine = bf16[8,256,128]{2,1,0:T(8,128)(2,1)S(1)} async-done(((bf16[8,256,128]{2,1,0:T(8,128)(2,1)}), bf16[8,256,128]{2,1,0:T(8,128)(2,1)S(1)}, u32[]{:S(2)}, u32[]{:S(2)}) %all-to-all-start.3) | async-done | bytes 524320 | tf_op jit(solution)/shard_map/all_to_all | solution.py:760
  72.8 1.8 %load.1 = (bf16[12,256,256]{2,1,0:T(8,128)(2,1)S(1)}, bf16[32,256,128]{2,1,0:T(8,128)(2,1)S(1)}) custom-call(s32[2048]{0:T(1024)S(4)} %settle.1.plan, bf16[32,256,256]{2,1,0:T(8,128)(2,1)} %bitcast.19, bf16[32,256,128]{2,1,0:T(8,128)(2,1)} %get-tuple-element.36.array), custom_call_target="tpu_custom_call" | custom-call | tf_op jit(solution)/shard_map/load/pallas_call | solution.py:547
  74.7 3.2 %last.1 = bf16[32,256,128]{2,1,0:T(8,128)(2,1)} custom-call(s32[2048]{0:T(1024)S(4)} %settle.1.plan, bf16[12,256,256]{2,1,0:T(8,128)(2,1)S(1)} %get-tuple-element.39.blocks, bf16[32,256,256]{2,1,0:T(8,128)(2,1)} %bitcast.20, bf16[32,256,256]{2,1,0:T(8,128)(2,1)} %collective-permute-done.4.tile_b, bf16[8,256,128]{2,1,0:T(8,128)(2,1)S(1)} %all-to-all-done.3.mine, ...), custom_call_target="tpu_custom_call" | custom-call | flops 536870912 | bytes 10485760 | tf_op jit(solution)/shard_map/last/pallas_call | solution.py:547
  (14 shorter events, 0.5 us)
Async XLA Ops:
  0.0 38.7 %collective-permute-start.4 = (bf16[32,256,256]{2,1,0:T(8,128)(2,1)}, bf16[32,256,256]{2,1,0:T(8,128)(2,1)}, u32[]{:S(2)}, u32[]{:S(2)}) collective-permute-start(bf16[32,256,256]{2,1,0:T(8,128)(2,1)} %bitcast.16), channel_id=1, source_target_pairs={{0,2},{2,0},{1,3},{3,1},{4,6},{6,4},{5,7},{7,5},{8,10},{10,8},{9,1... | collective-permute-start | bytes 12582920 | tf_op jit(solution)/shard_map/ppermute | solution.py:602
  16.1 2.1 %collective-permute-start.1 = (bf16[8,256,128]{2,1,0:T(8,128)(2,1)S(1)}, bf16[8,256,128]{2,1,0:T(8,128)(2,1)S(1)}, u32[]{:S(2)}, u32[]{:S(2)}) collective-permute-start(bf16[8,256,128]{2,1,0:T(8,128)(2,1)S(1)} %pick.1.picked), channel_id=1, source_target_pairs={{0,2},{2,0},{1,3},{3,1},{4,6},{6,4},{5,7},{7,5},{8,10},{10,8},{9,1... | collective-permute-start | bytes 1572872 | tf_op jit(solution)/shard_map/ppermute | solution.py:603
  16.8 2.2 %collective-permute-start = (s32[8,128]{1,0:T(8,128)S(1)}, s32[8,128]{1,0:T(8,128)S(1)}, u32[]{:S(2)}, u32[]{:S(2)}) collective-permute-start(s32[8,128]{1,0:T(8,128)S(1)} %bitcast.14), channel_id=1, source_target_pairs={{0,2},{2,0},{1,3},{3,1},{4,6},{6,4},{5,7},{7,5},{8,10},{10,8},{9,1... | collective-permute-start | bytes 12296 | tf_op jit(solution)/shard_map/ppermute | solution.py:604
  18.2 1.1 %collective-permute-start.2 = (s32[65]{0:T(128)S(1)}, s32[65]{0:T(128)S(1)}, u32[]{:S(2)}, u32[]{:S(2)}) collective-permute-start(s32[65]{0:T(128)S(1)} %pad_add_fusion.meta_a), channel_id=1, source_target_pairs={{0,2},{2,0},{1,3},{3,1},{4,6},{6,4},{5,7},{7,5},{8,10},{10,8},{9,1... | collective-permute-start | bytes 788 | tf_op jit(solution)/shard_map/ppermute | solution.py:606
  24.9 13.7 %all-to-all-start.1 = ((bf16[8,256,128]{2,1,0:T(8,128)(2,1)}), bf16[8,256,128]{2,1,0:T(8,128)(2,1)S(1)}, u32[]{:S(2)}, u32[]{:S(2)}) async-start(bf16[8,256,128]{2,1,0:T(8,128)(2,1)} %pack.1.start.previous), calls=%async_computation.1 | async-start | bytes 1048576 | tf_op jit(solution)/shard_map/all_to_all | solution.py:633
  28.4 1.4 %collective-permute-start.3 = (s32[2048]{0:T(1024)}, s32[2048]{0:T(1024)S(1)}, u32[]{:S(2)}, u32[]{:S(2)}) collective-permute-start(s32[2048]{0:T(1024)} %get-tuple-element.28), channel_id=1, source_target_pairs={{0,2},{2,0},{1,3},{3,1},{4,6},{6,4},{5,7},{7,5},{8,10},{10,8},{9,1... | collective-permute-start | bytes 24584 | tf_op jit(solution)/shard_map/ppermute | solution.py:637
  29.9 0.7 copy-start
  58.2 14.6 %all-to-all-start.3 = ((bf16[8,256,128]{2,1,0:T(8,128)(2,1)}), bf16[8,256,128]{2,1,0:T(8,128)(2,1)S(1)}, u32[]{:S(2)}, u32[]{:S(2)}) async-start(bf16[8,256,128]{2,1,0:T(8,128)(2,1)} %sent.3), calls=%async_computation.3 | async-start | bytes 1048576 | tf_op jit(solution)/shard_map/all_to_all | solution.py:760
  62.5 2.8 %collective-permute-start.5 = (bf16[8,256,128]{2,1,0:T(8,128)(2,1)S(1)}, bf16[8,256,128]{2,1,0:T(8,128)(2,1)S(1)}, u32[]{:S(2)}, u32[]{:S(2)}) collective-permute-start(bf16[8,256,128]{2,1,0:T(8,128)(2,1)S(1)} %all-to-all-done.1.pieces.q1), channel_id=1, source_target_pairs={{0,2},{2,0},{1,3},{3,1},{4,6},{6,4},{5,7},{7,5},{8,10},{10,8},{9,1... | collective-permute-start | bytes 1572872 | tf_op jit(solution)/shard_map/ppermute | solution.py:747
  62.5 2.8 %collective-permute-start.6 = (bf16[8,256,128]{2,1,0:T(8,128)(2,1)S(1)}, bf16[8,256,128]{2,1,0:T(8,128)(2,1)S(1)}, u32[]{:S(2)}, u32[]{:S(2)}) collective-permute-start(bf16[8,256,128]{2,1,0:T(8,128)(2,1)S(1)} %all_to_all.24.pieces.q2), channel_id=1, source_target_pairs={{0,2},{2,0},{1,3},{3,1},{4,6},{6,4},{5,7},{7,5},{8,10},{10,8},{9,1... | collective-permute-start | bytes 1572872 | tf_op jit(solution)/shard_map/ppermute | solution.py:748
  72.8 1.9 %collective-permute-start.7 = (bf16[8,256,128]{2,1,0:T(8,128)(2,1)S(1)}, bf16[8,256,128]{2,1,0:T(8,128)(2,1)S(1)}, u32[]{:S(2)}, u32[]{:S(2)}) collective-permute-start(bf16[8,256,128]{2,1,0:T(8,128)(2,1)S(1)} %all-to-all-done.3.mine), channel_id=1, source_target_pairs={{0,2},{2,0},{1,3},{3,1},{4,6},{6,4},{5,7},{7,5},{8,10},{10,8},{9,1... | collective-permute-start | bytes 1572872 | tf_op jit(solution)/shard_map/ppermute | solution.py:761

commit v5 on v4

--- a/solution.py
+++ b/solution.py
@@ -426,7 +426,7 @@
     own,
     blocks,
     sems,
-    row_sems,
+    row_sem,
 ):
     piece_blocks, block_size, width = base.shape
     begin, wait = fetches(plan, HEAD, STRIDE, 0, lay.slots, (tile_a, tile_b), blocks, sems)
@@ -438,7 +438,7 @@
         return pl.ds(pl.multiple_of(b * block_size, block_size), block_size)
 
     def put(b):
-        return pltpu.make_async_copy(own.at[rows(b)], base.at[b], row_sems.at[b])
+        return pltpu.make_async_copy(own.at[rows(b)], base.at[b], row_sem)
 
     add_products(
         plan,
@@ -459,9 +459,7 @@
         own[rows(b), :] = (-center_value * second - first).astype(jnp.bfloat16)
         put(b).start()
 
-    @pl.loop(0, piece_blocks)
-    def _(b):
-        put(b).wait()
+    pltpu.make_async_copy(base, base, row_sem).wait()
 
 
 def last_kernel(
@@ -711,7 +709,7 @@
                 VMEM(vectors.shape, jnp.bfloat16),
                 VMEM((2 * lay.slots, block_size, block_size), jnp.bfloat16),
                 DMA((2 * lay.slots,)),
-                DMA((piece_blocks,)),
+                DMA,
             ],
             18,
             "early",

time: 78.2 us -> 79.6 us (1.018)
  Pallas kernels: 25.1 us -> 28.8 us
  blocking collectives: 28.6 us -> 27.3 us
  waiting for transfers between devices: 11.7 us -> 10.9 us
    pallas_call x10, Pallas kernels: 25.1 us -> 28.8 us  [call(): pl.pallas_call(kernel, out_shape=[space(shape, dtype) for shape, dtype, s...]
    all_to_all x1, blocking collectives: 15.5 us -> 14.3 us  [on_pair(): q2 = exchange(first_sent)]
  transfers between devices with their start and end apart: 10 -> 10, of which waited for: 5 -> 5; matrix products, arithmetic and copies ran while one was open for 2% -> 2% of each run, Pallas kernels for 23% -> 24%
where the time goes in v5:
time: 79.6 us; the launch traced here: 79.2 us
  Pallas kernels  28.8 us (36%)
  blocking collectives  27.3 us (34%)
  waiting for transfers between devices  10.9 us (14%)
  starting transfers between devices  9.09 us (11%)
  other arithmetic  1.53 us (2%)
    pallas_call x10, Pallas kernels, call(): pl.pallas_call(kernel, out_shape=[space(shape, dtype) for shape, dtype, s...  28.8 us
    all_to_all x1, blocking collectives, on_pair(): q2 = exchange(first_sent)  14.3 us
    all_to_all x1, blocking collectives, on_pair(): wanted = exchange(jnp.broadcast_to(needed, (n_row, LANES)))  13.1 us
    all_to_all x1, waiting for transfers between devices, on_pair(): q1 = exchange(after(packed, own_list))  7.37 us
    all_to_all x1, starting transfers between devices, on_pair(): q3 = after(exchange(second_sent), base)  3.9 us
    all_to_all x1, starting transfers between devices, on_pair(): q1 = exchange(after(packed, own_list))  3.51 us
    all_to_all x1, waiting for transfers between devices, on_pair(): q3 = after(exchange(second_sent), base)  1.84 us
  transfers between devices with their start and end apart: 10, of which 5 were waited for; matrix products, arithmetic and copies ran while one was open for 2% of the time, Pallas kernels for 24%

profile of v5, /device:TPU:0, one launch (start us, length us, event | category | flops | bytes accessed | tf_op | source)
XLA Modules:
  0.0 79.2 jit_solution(13683358221488875774)
XLA Ops:
  0.0 0.5 collective-permute-start.4
  0.5 0.7 and_select_fusion.1
  1.3 13.1 %all_to_all.23 = s32[8,1,128]{2,1,0:T(1,128)S(1)} all-to-all(s32[8,1,128]{2,1,0:T(1,128)S(1)} %broadcast_in_dim.21), channel_id=1, replica_groups=mesh['row'=8,'col'=2,'vec'=2] {'row'}, dimensions={0} | all-to-all | bytes 8192 | tf_op jit(solution)/shard_map/all_to_all | solution.py:589
  14.4 1.7 %pick.1.picked = bf16[8,256,128]{2,1,0:T(8,128)(2,1)S(1)} custom-call(s32[8,128]{1,0:T(8,128)S(1)} %bitcast.13, bf16[8192,128]{1,0:T(8,128)(2,1)} %vectors.2), custom_call_target="tpu_custom_call" | custom-call | tf_op jit(solution)/shard_map/pick/pallas_call | solution.py:545
  16.8 0.6 collective-permute-start
  17.4 0.7 pad_add_fusion.meta_a
  18.2 0.9 %pack.1.start.previous = bf16[8,256,128]{2,1,0:T(8,128)(2,1)} custom-call(bf16[8,256,128]{2,1,0:T(8,128)(2,1)S(1)} %pick.1.picked, bf16[8,256,128]{2,1,0:T(8,128)(2,1)S(1)} %collective-permute-done.1.picked_b), custom_call_target="tpu_custom_call" | custom-call | tf_op jit(solution)/shard_map/pack/pallas_call | solution.py:545
  19.1 0.2 collective-permute-done.2.meta_b
  19.3 6.3 %plan.1 = (s32[2048]{0:T(1024)}, s32[2048]{0:T(1024)}) custom-call(s32[8,128]{1,0:T(8,128)S(1)} %bitcast.15, s32[8,128]{1,0:T(8,128)S(1)} %collective-permute-done.wanted_b, s32[65]{0:T(128)S(1)} %pad_add_fusion.meta_a, s32[65]{0:T(128)S(1)} %collective-permute-done.2.meta_b), custom_call_target="tpu_custom_call" | custom-call | tf_op jit(solution)/shard_map/plan/pallas_call | solution.py:545
  25.6 3.5 %all-to-all-start.1 = ((bf16[8,256,128]{2,1,0:T(8,128)(2,1)}), bf16[8,256,128]{2,1,0:T(8,128)(2,1)S(1)}, u32[]{:S(2)}, u32[]{:S(2)}) async-start(bf16[8,256,128]{2,1,0:T(8,128)(2,1)} %pack.1.start.previous), calls=%async_computation.1 | async-start | bytes 1048576 | tf_op jit(solution)/shard_map/all_to_all | solution.py:631
  29.1 1.4 %collective-permute-done.3.handed = s32[2048]{0:T(1024)S(1)} collective-permute-done((s32[2048]{0:T(1024)}, s32[2048]{0:T(1024)S(1)}, u32[]{:S(2)}, u32[]{:S(2)}) %collective-permute-start.3) | collective-permute-done | bytes 8224 | tf_op jit(solution)/shard_map/ppermute | solution.py:635
  30.5 0.7 copy-done
  31.2 0.7 settle.1.plan
  31.9 7.4 %all-to-all-done.1.pieces.q1 = bf16[8,256,128]{2,1,0:T(8,128)(2,1)S(1)} async-done(((bf16[8,256,128]{2,1,0:T(8,128)(2,1)}), bf16[8,256,128]{2,1,0:T(8,128)(2,1)S(1)}, u32[]{:S(2)}, u32[]{:S(2)}) %all-to-all-start.1) | async-done | bytes 524320 | tf_op jit(solution)/shard_map/all_to_all | solution.py:631
  39.3 3.2 %sent.2 = (bf16[8,256,128]{2,1,0:T(8,128)(2,1)S(1)}, bf16[66,256,256]{2,1,0:T(8,128)(2,1)S(1)}) custom-call(s32[2048]{0:T(1024)S(4)} %settle.1.plan, bf16[32,256,256]{2,1,0:T(8,128)(2,1)} %bitcast.17, bf16[32,256,256]{2,1,0:T(8,128)(2,1)} %collective-permute-done.4.tile_b, bf16[8,256,128]{2,1,0:T(8,128)(2,1)S(1)} %all-to-all-done.1.pieces.q1, ...), custom_call_target="tpu_custom_call" | custom-call | flops 134217728 | bytes 2621440 | tf_op jit(solution)/shard_map/sent/pallas_call | solution.py:545
  42.4 14.3 %all_to_all.24.pieces.q2 = bf16[8,256,128]{2,1,0:T(8,128)(2,1)S(1)} all-to-all(bf16[8,256,128]{2,1,0:T(8,128)(2,1)S(1)} %get-tuple-element.32.current), channel_id=1, replica_groups=mesh['row'=8,'col'=2,'vec'=2] {'row'}, dimensions={0} | all-to-all | bytes 1048576 | tf_op jit(solution)/shard_map/all_to_all | solution.py:743
  56.7 2.4 %sent.3 = bf16[8,256,128]{2,1,0:T(8,128)(2,1)} custom-call(s32[2048]{0:T(1024)S(4)} %settle.1.plan, bf16[66,256,256]{2,1,0:T(8,128)(2,1)S(1)} %get-tuple-element.31.blocks, bf16[8,256,128]{2,1,0:T(8,128)(2,1)S(1)} %all_to_all.24.pieces.q2, bf16[8,256,128]{2,1,0:T(8,128)(2,1)S(1)} %get-tuple-element.32.current, bf16[8,256,128]{2,1,0:T(8,128)(2,1)} %pack.1.start.previous), custom_call_target="tpu_custom_call" | custom-call | flops 134217728 | bytes 2621440 | tf_op jit(solution)/shard_map/sent/pallas_call | solution.py:545
  59.1 3.9 %all-to-all-start.3 = ((bf16[8,256,128]{2,1,0:T(8,128)(2,1)}), bf16[8,256,128]{2,1,0:T(8,128)(2,1)S(1)}, u32[]{:S(2)}, u32[]{:S(2)}) async-start(bf16[8,256,128]{2,1,0:T(8,128)(2,1)} %sent.3), calls=%async_computation.3 | async-start | bytes 1048576 | tf_op jit(solution)/shard_map/all_to_all | solution.py:758
  63.0 0.5 collective-permute-start.6
  63.6 2.3 %prime.1.start = f32[33,256,256]{2,1,0:T(8,128)S(1)} custom-call(bf16[8192,128]{1,0:T(8,128)(2,1)} %vectors.2), custom_call_target="tpu_custom_call" | custom-call | bytes 18874368 | tf_op jit(solution)/shard_map/prime/pallas_call | solution.py:545
  65.9 5.6 %early.1 = (bf16[32,256,128]{2,1,0:T(8,128)(2,1)}, f32[33,256,256]{2,1,0:T(8,128)S(1)}) custom-call(s32[2048]{0:T(1024)S(4)} %settle.1.plan, bf16[32,256,256]{2,1,0:T(8,128)(2,1)} %bitcast.18, bf16[32,256,256]{2,1,0:T(8,128)(2,1)} %collective-permute-done.4.tile_b, ...), custom_call_target="tpu_custom_call", output_to_operand_aliasing={{1}: (7, {})} | custom-call | flops 1073741824 | bytes 20971520 | tf_op jit(solution)/shard_map/early/pallas_call | solution.py:545
  71.5 1.8 %all-to-all-done.3.mine = bf16[8,256,128]{2,1,0:T(8,128)(2,1)S(1)} async-done(((bf16[8,256,128]{2,1,0:T(8,128)(2,1)}), bf16[8,256,128]{2,1,0:T(8,128)(2,1)S(1)}, u32[]{:S(2)}, u32[]{:S(2)}) %all-to-all-start.3) | async-done | bytes 524320 | tf_op jit(solution)/shard_map/all_to_all | solution.py:758
  73.3 1.8 %load.1 = (bf16[12,256,256]{2,1,0:T(8,128)(2,1)S(1)}, bf16[32,256,128]{2,1,0:T(8,128)(2,1)S(1)}) custom-call(s32[2048]{0:T(1024)S(4)} %settle.1.plan, bf16[32,256,256]{2,1,0:T(8,128)(2,1)} %bitcast.19, bf16[32,256,128]{2,1,0:T(8,128)(2,1)} %get-tuple-element.36.array), custom_call_target="tpu_custom_call" | custom-call | tf_op jit(solution)/shard_map/load/pallas_call | solution.py:545
  75.2 4.0 %last.1 = bf16[32,256,128]{2,1,0:T(8,128)(2,1)} custom-call(s32[2048]{0:T(1024)S(4)} %settle.1.plan, bf16[12,256,256]{2,1,0:T(8,128)(2,1)S(1)} %get-tuple-element.39.blocks, bf16[32,256,256]{2,1,0:T(8,128)(2,1)} %bitcast.20, bf16[32,256,256]{2,1,0:T(8,128)(2,1)} %collective-permute-done.4.tile_b, bf16[8,256,128]{2,1,0:T(8,128)(2,1)S(1)} %all-to-all-done.3.mine, ...), custom_call_target="tpu_custom_call" | custom-call | flops 536870912 | bytes 10485760 | tf_op jit(solution)/shard_map/last/pallas_call | solution.py:545
  (14 shorter events, 0.5 us)
Async XLA Ops:
  0.0 39.3 %collective-permute-start.4 = (bf16[32,256,256]{2,1,0:T(8,128)(2,1)}, bf16[32,256,256]{2,1,0:T(8,128)(2,1)}, u32[]{:S(2)}, u32[]{:S(2)}) collective-permute-start(bf16[32,256,256]{2,1,0:T(8,128)(2,1)} %bitcast.16), channel_id=1, source_target_pairs={{0,2},{2,0},{1,3},{3,1},{4,6},{6,4},{5,7},{7,5},{8,10},{10,8},{9,1... | collective-permute-start | bytes 12582920 | tf_op jit(solution)/shard_map/ppermute | solution.py:600
  16.1 2.1 %collective-permute-start.1 = (bf16[8,256,128]{2,1,0:T(8,128)(2,1)S(1)}, bf16[8,256,128]{2,1,0:T(8,128)(2,1)S(1)}, u32[]{:S(2)}, u32[]{:S(2)}) collective-permute-start(bf16[8,256,128]{2,1,0:T(8,128)(2,1)S(1)} %pick.1.picked), channel_id=1, source_target_pairs={{0,2},{2,0},{1,3},{3,1},{4,6},{6,4},{5,7},{7,5},{8,10},{10,8},{9,1... | collective-permute-start | bytes 1572872 | tf_op jit(solution)/shard_map/ppermute | solution.py:601
  16.8 2.2 %collective-permute-start = (s32[8,128]{1,0:T(8,128)S(1)}, s32[8,128]{1,0:T(8,128)S(1)}, u32[]{:S(2)}, u32[]{:S(2)}) collective-permute-start(s32[8,128]{1,0:T(8,128)S(1)} %bitcast.14), channel_id=1, source_target_pairs={{0,2},{2,0},{1,3},{3,1},{4,6},{6,4},{5,7},{7,5},{8,10},{10,8},{9,1... | collective-permute-start | bytes 12296 | tf_op jit(solution)/shard_map/ppermute | solution.py:602
  18.2 1.1 %collective-permute-start.2 = (s32[65]{0:T(128)S(1)}, s32[65]{0:T(128)S(1)}, u32[]{:S(2)}, u32[]{:S(2)}) collective-permute-start(s32[65]{0:T(128)S(1)} %pad_add_fusion.meta_a), channel_id=1, source_target_pairs={{0,2},{2,0},{1,3},{3,1},{4,6},{6,4},{5,7},{7,5},{8,10},{10,8},{9,1... | collective-permute-start | bytes 788 | tf_op jit(solution)/shard_map/ppermute | solution.py:604
  25.6 13.7 %all-to-all-start.1 = ((bf16[8,256,128]{2,1,0:T(8,128)(2,1)}), bf16[8,256,128]{2,1,0:T(8,128)(2,1)S(1)}, u32[]{:S(2)}, u32[]{:S(2)}) async-start(bf16[8,256,128]{2,1,0:T(8,128)(2,1)} %pack.1.start.previous), calls=%async_computation.1 | async-start | bytes 1048576 | tf_op jit(solution)/shard_map/all_to_all | solution.py:631
  29.1 1.4 %collective-permute-start.3 = (s32[2048]{0:T(1024)}, s32[2048]{0:T(1024)S(1)}, u32[]{:S(2)}, u32[]{:S(2)}) collective-permute-start(s32[2048]{0:T(1024)} %get-tuple-element.28), channel_id=1, source_target_pairs={{0,2},{2,0},{1,3},{3,1},{4,6},{6,4},{5,7},{7,5},{8,10},{10,8},{9,1... | collective-permute-start | bytes 24584 | tf_op jit(solution)/shard_map/ppermute | solution.py:635
  30.5 0.7 copy-start
  59.1 14.2 %all-to-all-start.3 = ((bf16[8,256,128]{2,1,0:T(8,128)(2,1)}), bf16[8,256,128]{2,1,0:T(8,128)(2,1)S(1)}, u32[]{:S(2)}, u32[]{:S(2)}) async-start(bf16[8,256,128]{2,1,0:T(8,128)(2,1)} %sent.3), calls=%async_computation.3 | async-start | bytes 1048576 | tf_op jit(solution)/shard_map/all_to_all | solution.py:758
  63.0 2.8 %collective-permute-start.5 = (bf16[8,256,128]{2,1,0:T(8,128)(2,1)S(1)}, bf16[8,256,128]{2,1,0:T(8,128)(2,1)S(1)}, u32[]{:S(2)}, u32[]{:S(2)}) collective-permute-start(bf16[8,256,128]{2,1,0:T(8,128)(2,1)S(1)} %all-to-all-done.1.pieces.q1), channel_id=1, source_target_pairs={{0,2},{2,0},{1,3},{3,1},{4,6},{6,4},{5,7},{7,5},{8,10},{10,8},{9,1... | collective-permute-start | bytes 1572872 | tf_op jit(solution)/shard_map/ppermute | solution.py:745
  63.0 2.8 %collective-permute-start.6 = (bf16[8,256,128]{2,1,0:T(8,128)(2,1)S(1)}, bf16[8,256,128]{2,1,0:T(8,128)(2,1)S(1)}, u32[]{:S(2)}, u32[]{:S(2)}) collective-permute-start(bf16[8,256,128]{2,1,0:T(8,128)(2,1)S(1)} %all_to_all.24.pieces.q2), channel_id=1, source_target_pairs={{0,2},{2,0},{1,3},{3,1},{4,6},{6,4},{5,7},{7,5},{8,10},{10,8},{9,1... | collective-permute-start | bytes 1572872 | tf_op jit(solution)/shard_map/ppermute | solution.py:746
  73.3 1.9 %collective-permute-start.7 = (bf16[8,256,128]{2,1,0:T(8,128)(2,1)S(1)}, bf16[8,256,128]{2,1,0:T(8,128)(2,1)S(1)}, u32[]{:S(2)}, u32[]{:S(2)}) collective-permute-start(bf16[8,256,128]{2,1,0:T(8,128)(2,1)S(1)} %all-to-all-done.3.mine), channel_id=1, source_target_pairs={{0,2},{2,0},{1,3},{3,1},{4,6},{6,4},{5,7},{7,5},{8,10},{10,8},{9,1... | collective-permute-start | bytes 1572872 | tf_op jit(solution)/shard_map/ppermute | solution.py:759
